TPU v7x, 32 devices: a whole 2x2x4 slice. The times are simulated.
32 devices in a mesh: seq: 8 (over z, core), ch: 4 (over y, x).
Axes of the slice: x: 2, y: 2, z: 4, core: 2. Of those that a mesh axis runs over, the one named last changes fastest.
Arguments:
- tokens: bfloat16 [8192, 4096], P('seq', 'ch'), may hold values from -6 to 6
- w_in: bfloat16 [4096, 3, 4096], P(None, None, 'ch'), may hold values from -0.09375 to 0.09375
- w_short: float32 [3, 3, 4096], P(None, None, 'ch'), may hold values from -3.5 to 3.5
- skip_gain: float32 [4096], P('ch'), may hold values from 0.5 to 1.5
- filter_spectra: bfloat16 [2, 16, 1024, 4096], P(None, 'seq', None, 'ch'), may hold values from -6 to 6
- w_out: bfloat16 [4096, 4096], P('ch'), may hold values from -0.09375 to 0.09375
Outputs:
- mixed_out: bfloat16 [8192, 4096], P(('seq', 'ch'))
All inputs are finite; a program needn't handle non-finite values.
Results may differ from a plain program's by a relative error of at most 0.015.
Values may be sent and summed in bfloat16 or wider, within the bound.
A program may use at most 256 MiB of HBM per device.

v0:
```python
import math

import jax
import jax.numpy as jnp
from jax import lax
from jax.sharding import PartitionSpec as P

TWO_PI = 2.0 * math.pi
TABLE_PRECISION = lax.Precision.HIGH


def shifted(array, axis, by):
    count = lax.axis_size(axis)
    pairs = [(i, i + by) for i in range(count) if 0 <= i + by < count]
    return lax.ppermute(array, axis, pairs)


def for_sending(array):
    return jax.tree.map(lambda a: a.astype(jnp.bfloat16) if a.dtype == jnp.float32 else a, array)


def phase_table(row_count, col_count, modulus):
    product = (
        jnp.arange(row_count, dtype=jnp.int32)[:, None]
        * jnp.arange(col_count, dtype=jnp.int32)[None, :]
        % modulus
    )
    phase_angle = product.astype(jnp.float32) * (TWO_PI / modulus)
    return (jnp.cos(phase_angle), jnp.sin(phase_angle))


def global_twiddle(freq_ids, pos_ids, fft_length):
    product = freq_ids[:, None] * pos_ids[None, :] % fft_length
    phase_angle = product.astype(jnp.float32) * (TWO_PI / fft_length)
    return (jnp.cos(phase_angle)[:, :, None], jnp.sin(phase_angle)[:, :, None])


def rotate(real_part, imag_part, cos_table, sin_table, orient):
    return (
        real_part * cos_table - orient * imag_part * sin_table,
        imag_part * cos_table + orient * real_part * sin_table,
    )


def transform(pattern, cos_table, sin_table, real_part, imag_part, orient):
    cos_real = jnp.einsum(pattern, cos_table, real_part, precision=TABLE_PRECISION)
    cos_imag = jnp.einsum(pattern, cos_table, imag_part, precision=TABLE_PRECISION)
    sin_real = jnp.einsum(pattern, sin_table, real_part, precision=TABLE_PRECISION)
    sin_imag = jnp.einsum(pattern, sin_table, imag_part, precision=TABLE_PRECISION)
    return (cos_real - orient * sin_imag, cos_imag + orient * sin_real)


def spectral_filter(real_part, imag_part, filter_spectra):
    bin_local, row_count, channels = real_part.shape
    outer_size = 32
    inner_size = row_count // outer_size
    cos_outer, sin_outer = phase_table(outer_size, outer_size, outer_size)
    cos_inner, sin_inner = phase_table(inner_size, inner_size, inner_size)
    cos_mid, sin_mid = phase_table(outer_size, inner_size, row_count)
    cos_mid = cos_mid[None, :, :, None]
    sin_mid = sin_mid[None, :, :, None]
    real_part = real_part.reshape(bin_local, outer_size, inner_size, channels)
    imag_part = imag_part.reshape(bin_local, outer_size, inner_size, channels)
    real_part, imag_part = transform(
        "kn,qnbc->qkbc", cos_outer, sin_outer, real_part, imag_part, -1.0
    )
    real_part, imag_part = rotate(real_part, imag_part, cos_mid, sin_mid, -1.0)
    real_part, imag_part = transform(
        "kn,qanc->qakc", cos_inner, sin_inner, real_part, imag_part, -1.0
    )
    response_table = filter_spectra.astype(jnp.float32).reshape(
        2, bin_local, inner_size, outer_size, channels
    )
    response_table = response_table.transpose(0, 1, 3, 2, 4)
    real_part, imag_part = (
        real_part * response_table[0] - imag_part * response_table[1],
        real_part * response_table[1] + imag_part * response_table[0],
    )
    real_part, imag_part = transform(
        "kn,qanc->qakc", cos_inner, sin_inner, real_part, imag_part, 1.0
    )
    real_part, imag_part = rotate(real_part, imag_part, cos_mid, sin_mid, 1.0)
    real_part, imag_part = transform(
        "kn,qnbc->qkbc", cos_outer, sin_outer, real_part, imag_part, 1.0
    )
    return (
        real_part.reshape(bin_local, row_count, channels),
        imag_part.reshape(bin_local, row_count, channels),
    )


def on_device(tokens, w_in, w_short, skip_gain, filter_spectra, w_out):
    row_count = tokens.shape[0]
    channels = w_in.shape[2]
    seq_count = lax.axis_size("seq")
    seq_pos = lax.axis_index("seq")
    bin_count = 2 * seq_count
    block_rows = row_count // seq_count
    fft_length = 2 * seq_count * row_count
    flat_in = w_in.reshape(w_in.shape[0], 3 * channels)
    projected = jnp.dot(
        lax.all_gather(tokens, "ch", axis=1, tiled=True),
        flat_in,
        preferred_element_type=jnp.float32,
    )
    projected = projected.astype(jnp.bfloat16).reshape(row_count, 3, channels)
    before = shifted(projected[row_count - 2 :], "seq", 1)
    extended = jnp.concatenate([before, projected], 0).astype(jnp.float32)
    streams = w_short[0] * extended[2:] + w_short[1] * extended[1:-1] + w_short[2] * extended[:-2]
    signal = (streams[:, 0] * streams[:, 2]).astype(jnp.bfloat16)
    local_bins = seq_pos * 2 + jnp.arange(2, dtype=jnp.int32)
    columns = lax.all_to_all(
        signal.reshape(1, row_count, channels), "seq", split_axis=1, concat_axis=0, tiled=True
    )
    cos_bins, sin_bins = phase_table(bin_count, seq_count, bin_count)
    real_part = jnp.einsum(
        "kp,pbc->kbc",
        cos_bins,
        columns,
        precision=TABLE_PRECISION,
        preferred_element_type=jnp.float32,
    )
    imag_part = -jnp.einsum(
        "kp,pbc->kbc",
        sin_bins,
        columns,
        precision=TABLE_PRECISION,
        preferred_element_type=jnp.float32,
    )
    block_ids = seq_pos * block_rows + jnp.arange(block_rows, dtype=jnp.int32)
    cos_twist, sin_twist = global_twiddle(
        jnp.arange(bin_count, dtype=jnp.int32), block_ids, fft_length
    )
    real_part, imag_part = rotate(real_part, imag_part, cos_twist, sin_twist, -1.0)
    spectrum = lax.all_to_all(
        jnp.stack([real_part, imag_part]).astype(jnp.bfloat16),
        "seq",
        split_axis=1,
        concat_axis=2,
        tiled=True,
    ).astype(jnp.float32)
    real_part, imag_part = (spectrum[0], spectrum[1])
    real_part, imag_part = spectral_filter(real_part, imag_part, filter_spectra)
    cos_twist, sin_twist = global_twiddle(
        local_bins, jnp.arange(row_count, dtype=jnp.int32), fft_length
    )
    real_part, imag_part = rotate(real_part, imag_part, cos_twist, sin_twist, 1.0)
    spectrum = lax.all_to_all(
        for_sending(jnp.stack([real_part, imag_part])),
        "seq",
        split_axis=2,
        concat_axis=1,
        tiled=True,
    )
    cos_back, sin_back = phase_table(seq_count, bin_count, bin_count)
    convolved = jnp.einsum("pk,kbc->pbc", cos_back, spectrum[0], precision=TABLE_PRECISION)
    convolved = convolved - jnp.einsum(
        "pk,kbc->pbc", sin_back, spectrum[1], precision=TABLE_PRECISION
    )
    convolved = convolved * (1.0 / fft_length)
    convolved = (
        lax.all_to_all(for_sending(convolved), "seq", split_axis=0, concat_axis=1, tiled=True)
        .astype(convolved.dtype)
        .reshape(row_count, channels)
    )
    response = convolved + skip_gain * signal.astype(jnp.float32)
    gated_out = (streams[:, 1] * response).astype(jnp.bfloat16)
    return lax.psum_scatter(
        jnp.dot(gated_out, w_out, preferred_element_type=jnp.float32).astype(jnp.bfloat16),
        "ch",
        scatter_dimension=0,
        tiled=True,
    )


def solution(mesh):
    return jax.shard_map(
        on_device,
        mesh=mesh,
        in_specs=(
            P("seq", "ch"),
            P(None, None, "ch"),
            P(None, None, "ch"),
            P("ch"),
            P(None, "seq", None, "ch"),
            P("ch", None),
        ),
        out_specs=P(("seq", "ch"), None),
        check_vma=False,
    )
```

profile of v0, /device:TPU:0, one launch (start us, length us, event | category | flops | bytes accessed | tf_op | source)
XLA Modules:
  0.0 1160.9 jit_solution(13380155396837873604)
XLA Ops:
  7.3 32.1 %copy.111 = bf16[4096,3,1024]{0,2,1:T(8,128)(2,1)} copy(bf16[4096,3,1024]{2,0,1:T(8,128)(2,1)} %param.7) | data formatting | bytes 50331648 | tf_op args[1]
  39.4 60.2 %all-gather.2.cloned.1.call-done = bf16[1024,4096]{1,0:T(8,128)(2,1)} async-done(((bf16[1024,1024]{1,0:T(8,128)(2,1)}), bf16[1024,4096]{1,0:T(8,128)(2,1)}) %all-gather.2.cloned.1.call-update) | async-done | bytes 8388624 | tf_op jit(solution)/shard_map/all_gather | solution.py:102
  99.5 32.0 %convolution_convert_fusion.1 = bf16[1024,3072]{1,0:T(8,128)(2,1)S(1)} fusion(bf16[1024,4096]{1,0:T(8,128)(2,1)} %all-gather.2.cloned.1.call-done, bf16[4096,3072]{0,1:T(8,128)(2,1)} %bitcast.180), kind=kOutput, calls=%fused_computation.52 | convolution fusion | flops 25772949504 | bytes 39845888 | tf_op jit(solution)/shard_map/dot_general | solution.py:101
  136.2 8.7 copy.112
  145.3 11.0 maximum_convert_fusion
  156.3 18.2 %fusion = f32[1024,3,1024]{0,2,1:T(8,128)S(1)} fusion(f32[1026,3,1024]{0,2,1:T(8,128)} %maximum_convert_fusion, f32[3,1024]{1,0:T(4,128)S(1)} %get-tuple-element.20, f32[3,1024]{1,0:T(4,128)S(1)} %get-tuple-element.21, f32[3,1024]{1,0:T(4,128)S(1)} %get-tuple-element.19), kind=kLoop, calls=%fused_computation.2 | loop fusion | flops 15728640 | bytes 50368512 | tf_op jit(solution)/shard_map/add | solution.py:109
  179.7 7.7 copy.115
  188.0 12.8 %reduce = bf16[1024,1024]{1,0:T(8,128)(2,1)S(1)} reduce(bf16[1024,1,1024]{2,1,0:T(2,128)(2,1)} %bitcast.184, bf16[]{:T(256)} %broadcast.433), dimensions={1}, to_apply=%bitcast.146.reduce_sub_computation | reduce | bytes 4194306
  204.5 5.3 all-to-all-start
  210.2 48.7 %all-to-all-done = bf16[8,2,65536]{2,1,0:T(2,128)(2,1)S(1)} async-done(((bf16[8,2,65536]{2,1,0:T(2,128)(2,1)}), bf16[8,2,65536]{2,1,0:T(2,128)(2,1)S(1)}, u32[]{:S(2)}, u32[]{:S(2)}) %all-to-all-start) | async-done | bytes 2097184 | tf_op jit(solution)/shard_map/all_to_all | solution.py:112
  269.0 6.7 fusion.22
  275.7 6.3 pad_maximum_fusion
  282.0 11.3 copy.120
  299.2 14.1 %copy.199 = f32[2,2,32,32,1024]{4,2,3,1,0:T(8,128)} copy(bf16[2,2,32,32,1024]{4,3,2,1,0:T(8,128)(2,1)} %bitcast.186) | data formatting | bytes 25165824 | tf_op jit(solution)/shard_map/transpose | solution.py:74
  313.5 168.6 %all-to-all-done.1 = bf16[2,16,128,1024]{3,2,0,1:T(8,128)(2,1)} async-done(((bf16[2,16,128,1024]{3,2,0,1:T(8,128)(2,1)}), bf16[2,16,128,1024]{3,2,0,1:T(8,128)(2,1)}, u32[]{:S(2)}, u32[]{:S(2)}) %all-to-all-start.1) | async-done | bytes 8388640 | tf_op jit(solution)/shard_map/all_to_all | solution.py:135
  482.2 8.2 copy.121
  495.1 5.0 fusion.30
  500.1 8.4 fusion.28
  511.1 9.1 multiply_subtract_fusion.1
  520.1 16.3 %fusion.4 = (f32[2,32,32,1024]{3,1,2,0:T(8,128)S(1)}, f32[2,32,32,1024]{3,1,2,0:T(8,128)}) fusion(f32[2,32,1024,32]{2,3,1,0:T(8,128)} %multiply_subtract_fusion.1, f32[32,32]{0,1:T(8,128)S(1)} %copy.129, f32[32,32]{0,1:T(8,128)S(1)} %copy.126, f32[2,32,1024,32]{2,3,1,0:T(8,128)} %fusion.28, bf16[2,32,32,1024]{3,2,1,0:T(8,128)(2,1)} %bitcast.172), kind=kOutput, calls=%fused_computation.18 | convolution fusion | flops 419444736 | bytes 37756928 | tf_op jit(solution)/shard_map/kn,qnbc->qkbc/dot_general | solution.py:48
  536.5 17.1 %fusion.16 = f32[2,32,1024,32]{2,3,1,0:T(8,128)S(1)} fusion(f32[2,32,32,1024]{3,1,2,0:T(8,128)} %get-tuple-element.12), kind=kOutput, calls=%fused_computation.44 | convolution fusion | flops 402667520 | bytes 16777216 | tf_op jit(solution)/shard_map/kn,qanc->qakc/dot_general | solution.py:49
  553.6 10.6 fusion.14
  564.2 11.4 multiply_subtract_fusion
  575.5 25.5 %fusion.2 = (f32[2,32,32,1024]{3,2,1,0:T(8,128)}, f32[2,32,32,1024]{3,2,1,0:T(8,128)}) fusion(f32[2,32,1024,32]{2,3,1,0:T(8,128)} %multiply_subtract_fusion, f32[2,2,32,32,1024]{4,3,2,1,0:T(8,128)} %bitcast.175, f32[2,32,1024,32]{2,3,1,0:T(8,128)} %fusion.14, f32[2,32,32,1024]{3,1,2,0:T(8,128)} %copy-done), kind=kOutput, calls=%fused_computation.12 | convolution fusion | flops 419444736 | bytes 58720256 | tf_op jit(solution)/shard_map/kn,qanc->qakc/dot_general | solution.py:48
  601.1 12.6 %fusion.63 = f32[2,32,1024,32]{2,3,1,0:T(8,128)} fusion(f32[2,32,32,1024]{3,2,1,0:T(8,128)} %get-tuple-element.8), kind=kOutput, calls=%fused_computation.93 | convolution fusion | flops 402667520 | bytes 16777216 | tf_op jit(solution)/shard_map/kn,qanc->qakc/dot_general | solution.py:49
  613.7 6.9 fusion.71
  620.6 6.8 fusion.61
  627.4 21.8 %subtract_bitcast_fusion.1 = (f32[2,32,32,1024]{3,2,1,0:T(8,128)}, f32[2,32,32,1024]{3,2,1,0:T(8,128)}) fusion(f32[32,32]{1,0:T(8,128)S(1)} %get-tuple-element.26, f32[32,32]{1,0:T(8,128)S(1)} %get-tuple-element.27, f32[2,32,1024,32]{2,3,1,0:T(8,128)} %fusion.71, f32[2,32,1024,32]{2,3,1,0:T(8,128)} %fusion.61, f32[2,32,1024,32]{2,3,1,0:T(8,128)} %fusion.63, ...), kind=kOutput, calls=%fused_computation.27 | convolution fusion | flops 419444736 | bytes 50339840 | tf_op jit(solution)/shard_map/kn,qanc->qakc/dot_general | solution.py:46
  649.2 16.8 %fusion.8 = f32[2,32,1024,32]{2,3,1,0:T(8,128)} fusion(f32[2,32,32,1024]{3,2,1,0:T(8,128)} %get-tuple-element.6), kind=kOutput, calls=%fused_computation.36 | convolution fusion | flops 402667520 | bytes 16777216 | tf_op jit(solution)/shard_map/kn,qnbc->qkbc/dot_general | solution.py:49
  666.1 10.5 fusion.6
  676.6 14.2 %subtract_bitcast_fusion = f32[2,32,32,1024]{3,1,2,0:T(8,128)} fusion(f32[2,32,1024,32]{2,3,1,0:T(8,128)} %fusion.8, f32[2,32,32,1024]{3,2,1,0:T(8,128)S(1)} %bitcast.168), kind=kOutput, calls=%fused_computation.25 | convolution fusion | flops 404764672 | bytes 25165824 | tf_op jit(solution)/shard_map/kn,qnbc->qkbc/dot_general | solution.py:46
  690.8 11.5 copy.137
  702.3 11.5 add_bitcast_fusion
  713.8 8.4 copy.140
  725.8 6.2 pad_maximum_fusion.1
  732.0 14.5 %copy.141 = bf16[2,2,1024,1024]{3,1,0,2:T(2,128)(2,1)S(1)} copy(bf16[2,2,1024,1024]{3,2,1,0:T(8,128)(2,1)} %pad_maximum_fusion.1) | data formatting | bytes 16777216 | tf_op jit(solution)/shard_map/stack | solution.py:149
  746.5 187.9 %all_to_all.51 = bf16[2,2,1024,1024]{3,1,0,2:T(2,128)(2,1)} all-to-all(bf16[2,2,1024,1024]{3,1,0,2:T(2,128)(2,1)S(1)} %copy.141), channel_id=1, replica_groups=mesh['seq'=8,'ch'=4] {'seq'}, dimensions={2} | all-to-all | bytes 16777216 | tf_op jit(solution)/shard_map/all_to_all | solution.py:148
  934.4 9.5 copy.142
  943.9 5.3 fusion.223
  949.2 6.4 copy.143
  955.5 7.4 squeeze.22
  963.0 5.6 fusion.124
  968.6 6.4 copy.144
  975.0 7.2 squeeze.23
  988.3 51.8 %all_to_all.52 = bf16[8,128,1024]{2,1,0:T(8,128)(2,1)S(1)} all-to-all(bf16[8,128,1024]{2,1,0:T(8,128)(2,1)S(1)} %copy.145), channel_id=1, replica_groups=mesh['seq'=8,'ch'=4] {'seq'}, dimensions={0} | all-to-all | bytes 4194304 | tf_op jit(solution)/shard_map/all_to_all | solution.py:162
  1042.7 5.4 copy.146
  1048.0 21.0 %convolution_convert_fusion = bf16[1024,4096]{1,0:T(8,128)(2,1)} fusion(bf16[1024,4096]{1,0:T(8,128)(2,1)} %param.11, f32[1024,3,1024]{0,2,1:T(8,128)} %copy-done.5, f32[1024,1024]{0,1:T(8,128)} %copy.146, f32[1024]{0:T(1024)S(1)} %copy-done.10), kind=kOutput, calls=%fused_computation.50 | convolution fusion | flops 8601468928 | bytes 33558528 | tf_op jit(solution)/shard_map/dot_general | solution.py:169
  1069.1 84.5 %reduce-scatter.2.cloned.1.call-done = bf16[256,4096]{1,0:T(8,128)(2,1)} async-done(((bf16[1024,4096]{1,0:T(8,128)(2,1)}), bf16[256,4096]{1,0:T(8,128)(2,1)}) %reduce-scatter.2.cloned.1.call-update) | async-done | bytes 2097168 | tf_op jit(solution)/shard_map/reduce_scatter | solution.py:168
  (66 shorter events, 51.3 us)
Async XLA Ops:
  6.5 93.0 %all-gather.2.cloned.1.call-start = ((), (), s32[]{:S(2)}) async-start(), calls=%async_computation.5 | async-start | bytes 10485760 | tf_op jit(solution)/shard_map/all_gather | solution.py:102
  99.5 36.6 %copy-start.9 = (f32[3,3,1024]{2,1,0:T(4,128)S(1)}, f32[3,3,1024]{2,1,0:T(4,128)}, u32[]{:S(2)}) copy-start(f32[3,3,1024]{2,1,0:T(4,128)} %param.8) | copy-start | bytes 110596
  131.5 2.6 copy-start.8
  134.2 10.7 collective-permute-start
  174.5 4.5 copy-start.5
  204.5 54.4 %all-to-all-start = ((bf16[8,2,65536]{2,1,0:T(2,128)(2,1)}), bf16[8,2,65536]{2,1,0:T(2,128)(2,1)S(1)}, u32[]{:S(2)}, u32[]{:S(2)}) async-start(bf16[8,2,65536]{2,1,0:T(2,128)(2,1)} %reshape.276), calls=%async_computation | async-start | bytes 4194304 | tf_op jit(solution)/shard_map/all_to_all | solution.py:112
  293.3 188.9 %all-to-all-start.1 = ((bf16[2,16,128,1024]{3,2,0,1:T(8,128)(2,1)}), bf16[2,16,128,1024]{3,2,0,1:T(8,128)(2,1)}, u32[]{:S(2)}, u32[]{:S(2)}) async-start(bf16[2,16,128,1024]{3,2,0,1:T(8,128)(2,1)} %copy.120), calls=%async_computation.1 | async-start | bytes 16777216 | tf_op jit(solution)/shard_map/all_to_all | solution.py:135
  298.3 855.3 %reduce-scatter.2.cloned.1.call-start = ((), (), s32[]{:S(2)}) async-start(), calls=%async_computation.6 | async-start | bytes 10485760 | tf_op jit(solution)/shard_map/reduce_scatter | solution.py:168
  509.1 2.0 copy-start.4
  536.5 27.7 %copy-start = (f32[2,32,32,1024]{3,1,2,0:T(8,128)}, f32[2,32,32,1024]{3,1,2,0:T(8,128)S(1)}, u32[]{:S(2)}) copy-start(f32[2,32,32,1024]{3,1,2,0:T(8,128)S(1)} %get-tuple-element.11) | copy-start | bytes 25165828
  536.5 17.1 %copy-start.2 = (f32[2,32,32,1024]{3,1,2,0:T(8,128)S(1)}, f32[2,32,32,1024]{3,1,2,0:T(8,128)}, u32[]{:S(2)}) copy-start(f32[2,32,32,1024]{3,1,2,0:T(8,128)} %get-tuple-element.12) | copy-start | bytes 25165828
  601.1 12.6 %copy-start.3 = (f32[2,32,32,1024]{3,2,1,0:T(8,128)S(1)}, f32[2,32,32,1024]{3,2,1,0:T(8,128)}, u32[]{:S(2)}) copy-start(f32[2,32,32,1024]{3,2,1,0:T(8,128)} %get-tuple-element.8) | copy-start | bytes 25165828
  601.1 19.5 %slice-start.2 = ((s8[8388608]{0:T(1024)(128)(4,1)}), s8[4194304]{0:T(1024)(128)(4,1)S(1)}, s32[]{:S(2)}) async-start(s8[8388608]{0:T(1024)(128)(4,1)} %bitcast.169), calls=%async_computation.9 | async-start | bytes 8388608
  613.7 6.9 slice-start.3
  649.2 16.9 %copy-start.1 = (f32[2,32,32,1024]{3,2,1,0:T(8,128)S(1)}, f32[2,32,32,1024]{3,2,1,0:T(8,128)}, u32[]{:S(2)}) copy-start(f32[2,32,32,1024]{3,2,1,0:T(8,128)} %get-tuple-element.6) | copy-start | bytes 25165828
  649.2 27.4 %slice-start = ((s8[8388608]{0:T(1024)(128)(4,1)}), s8[4194304]{0:T(1024)(128)(4,1)S(1)}, s32[]{:S(2)}) async-start(s8[8388608]{0:T(1024)(128)(4,1)} %bitcast.167), calls=%async_computation.7 | async-start | bytes 8388608
  666.1 10.5 slice-start.1
  713.8 8.4 copy-start.6
  963.0 5.6 copy-start.7
  1040.1 7.9 copy-start.10
Sparse Core Ops, SparseCore 0:
  9.2 90.2 all-gather.1
  1069.2 84.3 reduce-scatter.1
where the time goes:
time: 1170 us; the launch traced here: 1160 us
  waiting for transfers between devices  363 us (31%)
  matrix products  278 us (24%)
  blocking collectives  240 us (21%)
  local copies, waits for them, and re-layouts  192 us (16%)
  other arithmetic  61.7 us (5%)
  between operations  14.3 us (1%)
  starting transfers between devices  12.8 us (1%)
    all_to_all x1, blocking collectives, on_device(): lax.all_to_all(for_sending(jnp.stack([real_part, imag_part])), 'seq', spl...  188 us
    all_to_all x1, waiting for transfers between devices, on_device(): lax.all_to_all(jnp.stack([real_part, imag_part]).astype(jnp.bfloat16), 's...  169 us
    reduce_scatter x1, waiting for transfers between devices, on_device(): lax.psum_scatter(jnp.dot(gated_out, w_out, preferred_element_type=jnp.flo...  84.5 us
    dot_general x4, matrix products, transform(): jnp.einsum(pattern, sin_table, real_part, precision=TABLE_PRECISION)  60.2 us
    all_gather x1, waiting for transfers between devices, on_device(): lax.all_gather(tokens, 'ch', axis=1, tiled=True)  60.2 us
    dot_general x4, matrix products, transform(): jnp.einsum(pattern, cos_table, real_part, precision=TABLE_PRECISION)  56.4 us
    unnamed x35, local copies, waits for them, and re-layouts  52.9 us
    all_to_all x1, blocking collectives, on_device(): lax.all_to_all(for_sending(convolved), 'seq', split_axis=0, concat_axis=1...  51.8 us
  transfers between devices with their start and end apart: 5, of which 4 were waited for; matrix products, arithmetic and copies ran while one was open for 5% of the time, Pallas kernels for 0%

commit v1 on v0

v1 whole, which is shorter than its diff:
```python
import math

import jax
import jax.numpy as jnp
import ml_dtypes
import numpy as np
from jax import lax
from jax.sharding import PartitionSpec as P

TWO_PI = 2.0 * math.pi
BF16 = jnp.bfloat16
F32 = jnp.float32


def shifted(array, axis, by):
    count = lax.axis_size(axis)
    pairs = [(i, i + by) for i in range(count) if 0 <= i + by < count]
    return lax.ppermute(array, axis, pairs)


def dense_transform(size):
    product = np.outer(np.arange(size), np.arange(size)) % size
    angle = product * (TWO_PI / size)
    cos, sin = np.cos(angle), np.sin(angle)
    return np.block([[cos, sin], [-sin, cos]]).astype(ml_dtypes.bfloat16)


def phases(left, right, modulus):
    product = left[:, None] * right[None, :] % modulus
    angle = product.astype(F32) * (TWO_PI / modulus)
    return jnp.cos(angle), jnp.sin(angle)


def spread_filter(filter_spectra, seq_pos, seq_count):
    _, own, row_count, channels = filter_spectra.shape
    share = channels // seq_count
    pieces = []
    for k in range(seq_count):
        first = (seq_pos + k) % seq_count * share
        piece = lax.dynamic_slice_in_dim(filter_spectra, first, share, 3)
        if k:
            pairs = [(s, (s + k) % seq_count) for s in range(seq_count)]
            piece = lax.ppermute(piece, "seq", pairs)
        pieces.append(piece)
    return pieces


def on_device(tokens, w_in, w_short, skip_gain, filter_spectra, w_out):
    row_count = tokens.shape[0]
    channels = w_in.shape[2]
    seq_count = lax.axis_size("seq")
    seq_pos = lax.axis_index("seq")
    bin_count = 2 * seq_count
    share = channels // seq_count
    fft_length = bin_count * row_count

    pieces = spread_filter(filter_spectra, seq_pos, seq_count)

    gathered = lax.all_gather(tokens, "ch", axis=1, tiled=True)
    projected = [
        jnp.dot(gathered, w_in[:, s], preferred_element_type=F32).astype(BF16) for s in range(3)
    ]
    before = shifted(jnp.stack([p[row_count - 2 :] for p in projected]), "seq", 1)

    def stream(s):
        extended = jnp.concatenate([before[s], projected[s]], 0).astype(F32)
        taps = w_short[:, s]
        return taps[0] * extended[2:] + taps[1] * extended[1:-1] + taps[2] * extended[:-2]

    signal = (stream(0) * stream(2)).astype(BF16)
    second_gate = stream(1)

    columns = lax.all_to_all(
        signal.reshape(row_count, seq_count, share).transpose(1, 0, 2),
        "seq",
        split_axis=0,
        concat_axis=0,
        tiled=True,
    )
    senders = (seq_pos - jnp.arange(seq_count, dtype=jnp.int32)) % seq_count
    classes = (senders[:, None] * 2 + jnp.arange(2, dtype=jnp.int32)[None, :]).reshape(-1)
    cos_block, sin_block = phases(classes, jnp.arange(seq_count, dtype=jnp.int32), bin_count)
    cos_twist, sin_twist = phases(jnp.arange(row_count, dtype=jnp.int32), classes, fft_length)
    cos_twist, sin_twist = cos_twist[:, :, None], sin_twist[:, :, None]
    table = jnp.asarray(dense_transform(row_count))

    real = jnp.einsum("kp,pbc->bkc", cos_block.astype(BF16), columns, preferred_element_type=F32)
    imag = -jnp.einsum("kp,pbc->bkc", sin_block.astype(BF16), columns, preferred_element_type=F32)
    real, imag = (
        real * cos_twist + imag * sin_twist,
        imag * cos_twist - real * sin_twist,
    )
    packed = jnp.concatenate([real.astype(BF16), imag.astype(BF16)], 0)
    packed = packed.reshape(2 * row_count, bin_count * share)
    spectrum = jnp.dot(table, packed, preferred_element_type=F32).astype(BF16)
    spectrum = spectrum.reshape(2, row_count, bin_count, share).astype(F32)

    response = jnp.concatenate(pieces, 1).transpose(0, 2, 1, 3).astype(F32)
    real = spectrum[0] * response[0] - spectrum[1] * response[1]
    imag = spectrum[0] * response[1] + spectrum[1] * response[0]
    packed = jnp.concatenate([real.astype(BF16), imag.astype(BF16)], 0)
    packed = packed.reshape(2 * row_count, bin_count * share)
    partial = lax.dot_general(
        table, packed, (((0,), (0,)), ((), ())), preferred_element_type=F32
    ).astype(BF16)
    partial = partial.reshape(2, row_count, bin_count, share).astype(F32)
    scale = 1.0 / fft_length
    real = ((partial[0] * cos_twist - partial[1] * sin_twist) * scale).astype(BF16)
    imag = ((partial[1] * cos_twist + partial[0] * sin_twist) * scale).astype(BF16)
    convolved = jnp.einsum(
        "kp,bkc->pbc", cos_block.astype(BF16), real, preferred_element_type=F32
    ) - jnp.einsum("kp,bkc->pbc", sin_block.astype(BF16), imag, preferred_element_type=F32)
    convolved = lax.all_to_all(
        convolved.astype(BF16), "seq", split_axis=0, concat_axis=0, tiled=True
    )
    convolved = convolved.transpose(1, 0, 2).reshape(row_count, channels).astype(F32)

    response = convolved + skip_gain * signal.astype(F32)
    gated_out = (second_gate * response).astype(BF16)
    return lax.psum_scatter(
        jnp.dot(gated_out, w_out, preferred_element_type=F32).astype(BF16),
        "ch",
        scatter_dimension=0,
        tiled=True,
    )


def solution(mesh):
    return jax.shard_map(
        on_device,
        mesh=mesh,
        in_specs=(
            P("seq", "ch"),
            P(None, None, "ch"),
            P(None, None, "ch"),
            P("ch"),
            P(None, "seq", None, "ch"),
            P("ch", None),
        ),
        out_specs=P(("seq", "ch"), None),
        check_vma=False,
    )
```

time: 1170 us -> 733 us (0.63)
  blocking collectives: 240 us -> 0 us
  matrix products: 278 us -> 145 us
  local copies, waits for them, and re-layouts: 192 us -> 85.5 us
  starting transfers between devices: 12.8 us -> 103 us
  waiting for transfers between devices: 363 us -> 325 us
    all_to_all x2 -> x0, blocking collectives: 240 us -> none  [the longest x1 188 us: on_device(): lax.all_to_all(for_sending(jnp.stack([real_part, imag_part])), 'seq', spl...]
    all_to_all x2, waiting for transfers between devices: 217 us -> 44.9 us  [the longest x1 44.9 us: on_device(): lax.all_to_all(convolved.astype(BF16), 'seq', split_axis=0, concat_axis=0...]
    dot_general x22 -> x11, matrix products: 278 us -> 145 us  [the longest x3 37.8 us: on_device(): jnp.dot(gathered, w_in[:, s], preferred_element_type=F32).astype(BF16)]
    ppermute x0 -> x7, waiting for transfers between devices: none -> 102 us  [spread_filter(): piece = lax.ppermute(piece, 'seq', pairs)]
    all_to_all x2, starting transfers between devices: 10.3 us -> 74.4 us  [the longest x1 66.8 us: on_device(): lax.all_to_all(convolved.astype(BF16), 'seq', split_axis=0, concat_axis=0...]
    all_gather x1, waiting for transfers between devices: 60.2 us -> 92.3 us  [on_device(): gathered = lax.all_gather(tokens, 'ch', axis=1, tiled=True)]
    ppermute x0 -> x7, starting transfers between devices: none -> 27.1 us  [spread_filter(): piece = lax.ppermute(piece, 'seq', pairs)]
    another operation x2, local copies, waits for them, and re-layouts: 25.8 us -> 0.02 us  [on_device(): jnp.stack([p[row_count - 2:] for p in projected])]
  transfers between devices with their start and end apart: 5 -> 12, of which waited for: 4 -> 7; matrix products, arithmetic and copies ran while one was open for 5% -> 8% of each run, Pallas kernels for 0% -> 0%
where the time goes in v1:
time: 733 us; the launch traced here: 723 us
  waiting for transfers between devices  325 us (44%)
  matrix products  145 us (20%)
  starting transfers between devices  103 us (14%)
  local copies, waits for them, and re-layouts  85.5 us (12%)
  other arithmetic  51.3 us (7%)
  between operations  14.1 us (2%)
    ppermute x7, waiting for transfers between devices, spread_filter(): piece = lax.ppermute(piece, 'seq', pairs)  102 us
    all_gather x1, waiting for transfers between devices, on_device(): gathered = lax.all_gather(tokens, 'ch', axis=1, tiled=True)  92.3 us
    reduce_scatter x1, waiting for transfers between devices, on_device(): lax.psum_scatter(jnp.dot(gated_out, w_out, preferred_element_type=F32).as...  84.5 us
    all_to_all x1, starting transfers between devices, on_device(): lax.all_to_all(convolved.astype(BF16), 'seq', split_axis=0, concat_axis=0...  66.8 us
    all_to_all x1, waiting for transfers between devices, on_device(): lax.all_to_all(convolved.astype(BF16), 'seq', split_axis=0, concat_axis=0...  44.9 us
    dot_general x3, matrix products, on_device(): jnp.dot(gathered, w_in[:, s], preferred_element_type=F32).astype(BF16)  37.8 us
    unnamed x45, local copies, waits for them, and re-layouts  34.6 us
    dot_general x2, matrix products, on_device(): lax.dot_general(table, packed, (((0,), (0,)), ((), ())), preferred_elemen...  32.4 us
  transfers between devices with their start and end apart: 12, of which 7 were waited for; matrix products, arithmetic and copies ran while one was open for 8% of the time, Pallas kernels for 0%

profile of v1, /device:TPU:0, one launch (start us, length us, event | category | flops | bytes accessed | tf_op | source)
XLA Modules:
  0.0 723.4 jit_solution(9435017319297527586)
XLA Ops:
  7.3 92.3 %all-gather.2.cloned.1.call-done = bf16[1024,4096]{1,0:T(8,128)(2,1)} async-done(((bf16[1024,1024]{1,0:T(8,128)(2,1)}), bf16[1024,4096]{1,0:T(8,128)(2,1)}) %all-gather.2.cloned.1.call-update) | async-done | bytes 8388624 | tf_op jit(solution)/shard_map/all_gather | solution.py:59
  99.5 14.7 %fusion.39 = bf16[1024,1024]{1,0:T(8,128)(2,1)S(1)} fusion(bf16[1024,4096]{1,0:T(8,128)(2,1)} %all-gather.2.cloned.1.call-done, bf16[4096,3,1024]{2,0,1:T(8,128)(2,1)} %param.8), kind=kOutput, calls=%fused_computation.64 | convolution fusion | flops 8590983168 | bytes 18874368 | tf_op jit(solution)/shard_map/dot_general | solution.py:61
  114.3 11.2 %fusion.42 = bf16[1024,1024]{1,0:T(8,128)(2,1)S(1)} fusion(bf16[1024,4096]{1,0:T(8,128)(2,1)S(1)} %copy-done.12, bf16[4096,3,1024]{2,0,1:T(8,128)(2,1)} %param.8), kind=kOutput, calls=%fused_computation.65 | convolution fusion | flops 8590983168 | bytes 18874368 | tf_op jit(solution)/shard_map/dot_general | solution.py:61
  125.5 11.9 %fusion.45 = bf16[1024,1024]{1,0:T(8,128)(2,1)S(1)} fusion(bf16[1024,4096]{1,0:T(8,128)(2,1)S(1)} %copy-done.12, bf16[4096,3,1024]{2,0,1:T(8,128)(2,1)} %param.8), kind=kOutput, calls=%fused_computation.66 | convolution fusion | flops 8590983168 | bytes 18874368 | tf_op jit(solution)/shard_map/dot_general | solution.py:61
  138.8 1.7 collective-permute-start
  142.0 2.2 maximum_convert_fusion.2
  144.8 2.7 fusion.22
  148.9 1.8 bitcast_bitcast_fusion
  150.7 7.6 %all-to-all-start = ((bf16[8,1024,128]{2,1,0:T(8,128)(2,1)}), bf16[8,1024,128]{2,1,0:T(8,128)(2,1)S(1)}, u32[]{:S(2)}, u32[]{:S(2)}) async-start(bf16[8,1024,128]{2,1,0:T(8,128)(2,1)} %bitcast_bitcast_fusion), calls=%async_computation | async-start | bytes 4194304 | tf_op jit(solution)/shard_map/all_to_all | solution.py:73
  158.2 6.6 constant_dynamic-slice_fusion
  164.8 2.3 copy.46
  167.6 2.3 copy.47
  169.9 1.7 collective-permute-start.2
  171.6 2.3 copy.48
  173.9 2.2 collective-permute-start.3
  176.1 2.3 copy.49
  179.8 2.3 copy.50
  183.3 2.3 copy.45
  185.6 2.3 copy.51
  189.1 30.1 %collective-permute-done.1 = bf16[2,2,1024,128]{2,3,1,0:T(8,128)(2,1)} collective-permute-done((bf16[2,2,1024,128]{2,3,1,0:T(8,128)(2,1)}, bf16[2,2,1024,128]{2,3,1,0:T(8,128)(2,1)}, u32[]{:S(2)}, u32[]{:S(2)}) %collective-permute-start.1) | collective-permute-done | bytes 1048608 | tf_op jit(solution)/shard_map/ppermute | solution.py:43
  219.8 2.3 constant_dynamic-update-slice_fusion.7
  222.1 19.6 %collective-permute-start.7 = (bf16[2,2,1024,128]{2,3,1,0:T(8,128)(2,1)}, bf16[2,2,1024,128]{2,3,1,0:T(8,128)(2,1)S(1)}, u32[]{:S(2)}, u32[]{:S(2)}) collective-permute-start(bf16[2,2,1024,128]{2,3,1,0:T(8,128)(2,1)} %copy.52), channel_id=1, source_target_pairs={{0,28},{4,0},{8,4},{12,8},{16,12},{20,16},{24,20},{28,24},{1,29},{... | collective-permute-start | bytes 3145736 | tf_op jit(solution)/shard_map/ppermute | solution.py:43
  241.7 2.1 fusion.59
  243.8 2.3 constant_dynamic-update-slice_fusion.6
  246.0 2.2 constant_dynamic-update-slice_fusion.5
  248.3 71.0 %collective-permute-done.3 = bf16[2,2,1024,128]{2,3,1,0:T(8,128)(2,1)} collective-permute-done((bf16[2,2,1024,128]{2,3,1,0:T(8,128)(2,1)}, bf16[2,2,1024,128]{2,3,1,0:T(8,128)(2,1)}, u32[]{:S(2)}, u32[]{:S(2)}) %collective-permute-start.3) | collective-permute-done | bytes 1048608 | tf_op jit(solution)/shard_map/ppermute | solution.py:43
  319.3 2.3 constant_dynamic-update-slice_fusion.4
  321.6 2.3 constant_dynamic-update-slice_fusion.3
  323.8 2.2 constant_dynamic-update-slice_fusion.2
  329.2 11.3 %convert_bitcast_fusion.1 = f32[2,1024,16,128]{1,3,2,0:T(8,128)} fusion(bf16[2,16,1024,128]{2,3,1,0:T(8,128)(2,1)} %constant_dynamic-update-slice_fusion), kind=kLoop, calls=%fused_computation.1 | loop fusion | flops 4194304 | bytes 25165824 | tf_op jit(solution)/shard_map/convert_element_type | solution.py:98
  342.1 10.2 %fusion.14 = (bf16[1024,16,128]{2,1,0:T(8,128)(2,1)S(1)}, bf16[1024,16,128]{2,1,0:T(8,128)(2,1)S(1)}) fusion(f32[1024,128,16]{1,2,0:T(8,128)S(1)} %fusion.48, f32[1024,16]{1,0:T(8,128)S(1)} %get-tuple-element.34, f32[1024,16]{1,0:T(8,128)S(1)} %get-tuple-element.33, s32[16]{0:T(128)S(1)} %add.164, bf16[8,1024,128]{2,1,0:T(8,128)(2,1)S(1)} %all-to-all-done), kind=kOutput, calls=%fused_computation.24 | convolution fusion | flops 52430720 | bytes 19005504 | tf_op jit(solution)/shard_map/kp,pbc->bkc/dot_general | solution.py:87
  352.3 14.7 %pad_maximum_fusion = bf16[2048,16,128]{2,1,0:T(8,128)(2,1)S(1)} fusion(bf16[1024,16,128]{2,1,0:T(8,128)(2,1)S(1)} %get-tuple-element.8, bf16[1024,16,128]{2,1,0:T(8,128)(2,1)S(1)} %get-tuple-element.7), kind=kLoop, calls=%fused_computation.7 | loop fusion | flops 4194304 | bytes 16777216 | tf_op jit(solution)/shard_map/concatenate | solution.py:93
  367.0 23.5 %convert_bitcast_fusion.2 = f32[2048,2048]{0,1:T(8,128)} fusion(bf16[2048,2048]{1,0:T(8,128)(2,1)} %constant.110.clone, bf16[256,8,16,128]{3,2,1,0:T(8,128)(2,1)S(1)} %bitcast.100), kind=kOutput, calls=%fused_computation.2 | convolution fusion | flops 17188257792 | bytes 33554432 | tf_op jit(solution)/shard_map/dot_general | solution.py:95
  390.5 9.2 %fusion.93 = (f32[1024,2048]{0,1:T(8,128)S(1)}, f32[1024,2048]{0,1:T(8,128)}) fusion(f32[2048,2048]{0,1:T(8,128)} %convert_bitcast_fusion.2), kind=kLoop, calls=%fused_computation.143 | loop fusion | bytes 33554432 | tf_op jit(solution)/shard_map/slice | solution.py:99
  399.7 13.3 %subtract_convert_fusion = (bf16[1,1024,16,128]{1,3,2,0:T(8,128)(2,1)}, bf16[1,1024,16,128]{1,3,2,0:T(8,128)(2,1)}) fusion(f32[1,1024,16,128]{1,3,2,0:T(8,128)} %bitcast.97, f32[1,1024,16,128]{1,3,2,0:T(8,128)S(1)} %bitcast.96, f32[2,1024,16,128]{1,3,2,0:T(8,128)} %convert_bitcast_fusion.1), kind=kLoop, calls=%fused_computation.17 | loop fusion | flops 16777216 | bytes 41943040 | tf_op jit(solution)/shard_map/convert_element_type | solution.py:101
  413.1 15.3 %fusion.99 = f32[2048,2048]{1,0:T(8,128)} fusion(bf16[1024,2048]{0,1:T(8,128)(2,1)} %bitcast.102, bf16[1024,2048]{1,0:T(8,128)(2,1)} %constant.113), kind=kOutput, calls=%fused_computation.145 | convolution fusion | flops 8589934592 | bytes 25165824 | tf_op jit(solution)/shard_map/dot_general | solution.py:103
  428.3 17.1 %convert_bitcast_fusion = f32[2048,2048]{0,1:T(8,128)} fusion(f32[2048,2048]{1,0:T(8,128)} %fusion.99, bf16[1024,2048]{0,1:T(8,128)(2,1)S(1)} %bitcast.101, bf16[1024,2048]{1,0:T(8,128)(2,1)S(1)} %copy-done.14), kind=kOutput, calls=%fused_computation | convolution fusion | flops 8602517504 | bytes 41943040 | tf_op jit(solution)/shard_map/dot_general | solution.py:103
  445.4 10.9 %fusion.92 = (f32[1024,2048]{0,1:T(8,128)}, f32[1024,2048]{0,1:T(8,128)}) fusion(f32[2048,2048]{0,1:T(8,128)} %convert_bitcast_fusion), kind=kLoop, calls=%fused_computation.142 | loop fusion | bytes 33554432 | tf_op jit(solution)/shard_map/slice | solution.py:108
  456.3 9.2 %copy.40 = f32[1024,16,128]{2,1,0:T(8,128)} copy(f32[1024,16,128]{0,2,1:T(8,128)} %bitcast.99) | data formatting | bytes 16777216 | tf_op jit(solution)/shard_map/squeeze | solution.py:108
  465.5 9.2 %copy.39 = f32[1024,16,128]{2,1,0:T(8,128)} copy(f32[1024,16,128]{0,2,1:T(8,128)} %bitcast.98) | data formatting | bytes 16777216 | tf_op jit(solution)/shard_map/squeeze | solution.py:108
  474.7 12.4 %fusion.16 = f32[8,1024,128]{2,0,1:T(8,128)S(1)} fusion(f32[1024,16,128]{2,1,0:T(8,128)} %copy.40, f32[1024,16,128]{2,1,0:T(8,128)} %copy.39, f32[1024,16]{1,0:T(8,128)S(1)} %get-tuple-element.34, f32[1024,16]{1,0:T(8,128)S(1)} %get-tuple-element.33, s32[16]{0:T(128)S(1)} %add.164), kind=kOutput, calls=%fused_computation.26 | convolution fusion | flops 44042112 | bytes 21102656 | tf_op jit(solution)/shard_map/kp,bkc->pbc/dot_general | solution.py:110
  487.1 6.1 subtract_convert_fusion.2
  493.2 1.7 copy.43
  494.9 66.8 %all-to-all-start.1 = ((bf16[8,1024,128]{2,1,0:T(8,128)(2,1)}), bf16[8,1024,128]{2,1,0:T(8,128)(2,1)}, u32[]{:S(2)}, u32[]{:S(2)}) async-start(bf16[8,1024,128]{2,1,0:T(8,128)(2,1)} %copy.43), calls=%async_computation.1 | async-start | bytes 4194304 | tf_op jit(solution)/shard_map/all_to_all | solution.py:113
  561.8 4.2 maximum_convert_fusion
  566.0 44.9 %all-to-all-done.1 = bf16[8,1024,128]{2,1,0:T(8,128)(2,1)} async-done(((bf16[8,1024,128]{2,1,0:T(8,128)(2,1)}), bf16[8,1024,128]{2,1,0:T(8,128)(2,1)}, u32[]{:S(2)}, u32[]{:S(2)}) %all-to-all-start.1) | async-done | bytes 2097184 | tf_op jit(solution)/shard_map/all_to_all | solution.py:113
  610.9 20.7 %convolution_convert_fusion = bf16[1024,4096]{1,0:T(8,128)(2,1)} fusion(bf16[1024,4096]{1,0:T(8,128)(2,1)} %param.12, f32[1026,1024]{1,0:T(8,128)} %maximum_convert_fusion, bf16[1024,1024]{1,0:T(8,128)(2,1)S(1)} %copy-done.3, f32[1024]{0:T(1024)S(1)} %copy-done.13, f32[1024]{0:T(1024)S(1)} %bitcast.110, f32[1024]{0:T(1024)S(1)} %bitcast.111, ...), kind=kOutput, calls=%fused_computation.23 | convolution fusion | flops 8605663232 | bytes 33570816 | tf_op jit(solution)/shard_map/dot_general | solution.py:121
  631.6 84.5 %reduce-scatter.2.cloned.1.call-done = bf16[256,4096]{1,0:T(8,128)(2,1)} async-done(((bf16[1024,4096]{1,0:T(8,128)(2,1)}), bf16[256,4096]{1,0:T(8,128)(2,1)}) %reduce-scatter.2.cloned.1.call-update) | async-done | bytes 2097168 | tf_op jit(solution)/shard_map/reduce_scatter | solution.py:120
  (58 shorter events, 15.3 us)
Async XLA Ops:
  6.5 93.0 %all-gather.2.cloned.1.call-start = ((), (), s32[]{:S(2)}) async-start(), calls=%async_computation.3 | async-start | bytes 10485760 | tf_op jit(solution)/shard_map/all_gather | solution.py:59
  99.5 14.7 %copy-start.12 = (bf16[1024,4096]{1,0:T(8,128)(2,1)S(1)}, bf16[1024,4096]{1,0:T(8,128)(2,1)}, u32[]{:S(2)}) copy-start(bf16[1024,4096]{1,0:T(8,128)(2,1)} %all-gather.2.cloned.1.call-done) | copy-start | bytes 25165828
  125.5 12.0 %copy-start.5 = (bf16[1024,1024]{1,0:T(8,128)(2,1)}, bf16[1024,1024]{1,0:T(8,128)(2,1)S(1)}, u32[]{:S(2)}) copy-start(bf16[1024,1024]{1,0:T(8,128)(2,1)S(1)} %fusion.42) | copy-start | bytes 6291460
  125.5 15.1 %copy-start.7 = (f32[3,3,1024]{2,1,0:T(4,128)S(1)}, f32[3,3,1024]{2,1,0:T(4,128)}, u32[]{:S(2)}) copy-start(f32[3,3,1024]{2,1,0:T(4,128)} %param.9) | copy-start | bytes 110596
  137.4 1.4 copy-start.6
  138.8 2.6 collective-permute-start
  147.5 1.4 copy-start.2
  150.7 189.8 %all-to-all-start = ((bf16[8,1024,128]{2,1,0:T(8,128)(2,1)}), bf16[8,1024,128]{2,1,0:T(8,128)(2,1)S(1)}, u32[]{:S(2)}, u32[]{:S(2)}) async-start(bf16[8,1024,128]{2,1,0:T(8,128)(2,1)} %bitcast_bitcast_fusion), calls=%async_computation | async-start | bytes 4194304 | tf_op jit(solution)/shard_map/all_to_all | solution.py:73
  167.1 52.2 %collective-permute-start.1 = (bf16[2,2,1024,128]{2,3,1,0:T(8,128)(2,1)}, bf16[2,2,1024,128]{2,3,1,0:T(8,128)(2,1)}, u32[]{:S(2)}, u32[]{:S(2)}) collective-permute-start(bf16[2,2,1024,128]{2,3,1,0:T(8,128)(2,1)} %copy.46), channel_id=1, source_target_pairs={{0,4},{4,8},{8,12},{12,16},{16,20},{20,24},{24,28},{28,0},{1,5},{5... | collective-permute-start | bytes 3145736 | tf_op jit(solution)/shard_map/ppermute | solution.py:43
  169.9 52.2 %collective-permute-start.2 = (bf16[2,2,1024,128]{2,3,1,0:T(8,128)(2,1)}, bf16[2,2,1024,128]{2,3,1,0:T(8,128)(2,1)}, u32[]{:S(2)}, u32[]{:S(2)}) collective-permute-start(bf16[2,2,1024,128]{2,3,1,0:T(8,128)(2,1)} %copy.47), channel_id=1, source_target_pairs={{0,8},{4,12},{8,16},{12,20},{16,24},{20,28},{24,0},{28,4},{1,9},{5... | collective-permute-start | bytes 3145736 | tf_op jit(solution)/shard_map/ppermute | solution.py:43
  173.9 145.4 %collective-permute-start.3 = (bf16[2,2,1024,128]{2,3,1,0:T(8,128)(2,1)}, bf16[2,2,1024,128]{2,3,1,0:T(8,128)(2,1)}, u32[]{:S(2)}, u32[]{:S(2)}) collective-permute-start(bf16[2,2,1024,128]{2,3,1,0:T(8,128)(2,1)} %copy.48), channel_id=1, source_target_pairs={{0,12},{4,16},{8,20},{12,24},{16,28},{20,0},{24,4},{28,8},{1,13},{... | collective-permute-start | bytes 3145736 | tf_op jit(solution)/shard_map/ppermute | solution.py:43
  178.4 143.2 %collective-permute-start.4 = (bf16[2,2,1024,128]{2,3,1,0:T(8,128)(2,1)}, bf16[2,2,1024,128]{2,3,1,0:T(8,128)(2,1)}, u32[]{:S(2)}, u32[]{:S(2)}) collective-permute-start(bf16[2,2,1024,128]{2,3,1,0:T(8,128)(2,1)} %copy.49), channel_id=1, source_target_pairs={{0,16},{4,20},{8,24},{12,28},{16,0},{20,4},{24,8},{28,12},{1,17},{... | collective-permute-start | bytes 3145736 | tf_op jit(solution)/shard_map/ppermute | solution.py:43
  182.1 141.8 %collective-permute-start.5 = (bf16[2,2,1024,128]{2,3,1,0:T(8,128)(2,1)}, bf16[2,2,1024,128]{2,3,1,0:T(8,128)(2,1)}, u32[]{:S(2)}, u32[]{:S(2)}) collective-permute-start(bf16[2,2,1024,128]{2,3,1,0:T(8,128)(2,1)} %copy.50), channel_id=1, source_target_pairs={{0,20},{4,24},{8,28},{12,0},{16,4},{20,8},{24,12},{28,16},{1,21},{... | collective-permute-start | bytes 3145736 | tf_op jit(solution)/shard_map/ppermute | solution.py:43
  219.3 106.8 %collective-permute-start.6 = (bf16[2,2,1024,128]{2,3,1,0:T(8,128)(2,1)}, bf16[2,2,1024,128]{2,3,1,0:T(8,128)(2,1)S(1)}, u32[]{:S(2)}, u32[]{:S(2)}) collective-permute-start(bf16[2,2,1024,128]{2,3,1,0:T(8,128)(2,1)} %copy.51), channel_id=1, source_target_pairs={{0,24},{4,28},{8,0},{12,4},{16,8},{20,12},{24,16},{28,20},{1,25},{... | collective-permute-start | bytes 3145736 | tf_op jit(solution)/shard_map/ppermute | solution.py:43
  222.1 105.9 %collective-permute-start.7 = (bf16[2,2,1024,128]{2,3,1,0:T(8,128)(2,1)}, bf16[2,2,1024,128]{2,3,1,0:T(8,128)(2,1)S(1)}, u32[]{:S(2)}, u32[]{:S(2)}) collective-permute-start(bf16[2,2,1024,128]{2,3,1,0:T(8,128)(2,1)} %copy.52), channel_id=1, source_target_pairs={{0,28},{4,0},{8,4},{12,8},{16,12},{20,16},{24,20},{28,24},{1,29},{... | collective-permute-start | bytes 3145736 | tf_op jit(solution)/shard_map/ppermute | solution.py:43
  413.1 15.3 %copy-start.4 = (bf16[1,1024,16,128]{1,3,2,0:T(8,128)(2,1)S(1)}, bf16[1,1024,16,128]{1,3,2,0:T(8,128)(2,1)}, u32[]{:S(2)}) copy-start(bf16[1,1024,16,128]{1,3,2,0:T(8,128)(2,1)} %get-tuple-element.5) | copy-start | bytes 12582916
  413.1 15.3 %copy-start.14 = (bf16[1024,2048]{1,0:T(8,128)(2,1)S(1)}, bf16[1024,2048]{1,0:T(8,128)(2,1)}, u32[]{:S(2)}) copy-start(bf16[1024,2048]{1,0:T(8,128)(2,1)} %constant.112) | copy-start | bytes 12582916
  474.7 12.4 %copy-start = (f32[1024,16,128]{2,1,0:T(8,128)S(1)}, f32[1024,16,128]{2,1,0:T(8,128)}, u32[]{:S(2)}) copy-start(f32[1024,16,128]{2,1,0:T(8,128)} %copy.40) | copy-start | bytes 25165828
  474.7 12.4 %copy-start.1 = (f32[1024,16,128]{2,1,0:T(8,128)S(1)}, f32[1024,16,128]{2,1,0:T(8,128)}, u32[]{:S(2)}) copy-start(f32[1024,16,128]{2,1,0:T(8,128)} %copy.39) | copy-start | bytes 25165828
  493.2 68.6 %copy-start.8 = (bf16[2,1024]{1,0:T(2,128)(2,1)S(1)}, bf16[2,1024]{1,0:T(2,128)(2,1)}, u32[]{:S(2)}) copy-start(bf16[2,1024]{1,0:T(2,128)(2,1)} %get-tuple-element.30) | copy-start | bytes 12292
  494.9 116.0 %copy-start.3 = (bf16[1024,1024]{1,0:T(8,128)(2,1)S(1)}, bf16[1024,1024]{1,0:T(8,128)(2,1)}, u32[]{:S(2)}) copy-start(bf16[1024,1024]{1,0:T(8,128)(2,1)} %copy-done.2) | copy-start | bytes 6291460
  494.9 116.0 %copy-start.9 = (f32[1,1,1024]{2,1,0:T(1,128)S(1)}, f32[1,1,1024]{2,1,0:T(1,128)}, u32[]{:S(2)}) copy-start(f32[1,1,1024]{2,1,0:T(1,128)} %get-tuple-element.21) | copy-start | bytes 12292
  494.9 116.0 %copy-start.10 = (f32[1,1,1024]{2,1,0:T(1,128)S(1)}, f32[1,1,1024]{2,1,0:T(1,128)}, u32[]{:S(2)}) copy-start(f32[1,1,1024]{2,1,0:T(1,128)} %get-tuple-element.26) | copy-start | bytes 12292
  494.9 116.0 %copy-start.11 = (f32[1,1,1024]{2,1,0:T(1,128)S(1)}, f32[1,1,1024]{2,1,0:T(1,128)}, u32[]{:S(2)}) copy-start(f32[1,1,1024]{2,1,0:T(1,128)} %get-tuple-element.27) | copy-start | bytes 12292
  494.9 116.0 %copy-start.13 = (f32[1024]{0:T(1024)S(1)}, f32[1024]{0:T(1024)}, u32[]{:S(2)}) copy-start(f32[1024]{0:T(1024)} %param.10) | copy-start | bytes 12292
  494.9 116.0 %all-to-all-start.1 = ((bf16[8,1024,128]{2,1,0:T(8,128)(2,1)}), bf16[8,1024,128]{2,1,0:T(8,128)(2,1)}, u32[]{:S(2)}, u32[]{:S(2)}) async-start(bf16[8,1024,128]{2,1,0:T(8,128)(2,1)} %copy.43), calls=%async_computation.1 | async-start | bytes 4194304 | tf_op jit(solution)/shard_map/all_to_all | solution.py:113
  561.7 154.4 %reduce-scatter.2.cloned.1.call-start = ((), (), s32[]{:S(2)}) async-start(), calls=%async_computation.4 | async-start | bytes 10485760 | tf_op jit(solution)/shard_map/reduce_scatter | solution.py:120
Sparse Core Ops, SparseCore 0:
  9.2 90.2 all-gather.1
  631.7 84.3 reduce-scatter.1

commit v2 on v1

--- a/solution.py
+++ b/solution.py
@@ -5,6 +5,8 @@
 import ml_dtypes
 import numpy as np
 from jax import lax
+from jax.experimental import pallas as pl
+from jax.experimental.pallas import tpu as pltpu
 from jax.sharding import PartitionSpec as P
 
 TWO_PI = 2.0 * math.pi
@@ -45,6 +47,98 @@
     return pieces
 
 
+def long_filter(cos_ref, sin_ref, x_ref, ct_ref, st_ref, h_ref, table_ref, out_ref, acc, left, right):
+    blocks, row_count, share = x_ref.shape
+    step = pl.program_id(0)
+    chunk, tile = 64, 512
+
+    @pl.when(step == 0)
+    def _():
+        acc[...] = jnp.zeros_like(acc)
+
+    @pl.loop(0, row_count // chunk)
+    def _(c):
+        rows = pl.ds(pl.multiple_of(c * chunk, chunk), chunk)
+        below = pl.ds(pl.multiple_of(row_count + c * chunk, chunk), chunk)
+        x = [x_ref[p, rows, :].astype(F32) for p in range(blocks)]
+        for q in range(2):
+            real = x[0]
+            imag = jnp.zeros_like(real)
+            for p in range(1, blocks):
+                real = real + cos_ref[2 * step + q, p] * x[p]
+                imag = imag - sin_ref[2 * step + q, p] * x[p]
+            ct, st = ct_ref[q, rows, :], st_ref[q, rows, :]
+            lanes = slice(q * share, (q + 1) * share)
+            left[rows, lanes] = (real * ct + imag * st).astype(BF16)
+            left[below, lanes] = (imag * ct - real * st).astype(BF16)
+
+    @pl.loop(0, row_count // tile)
+    def _(m):
+        rows = pl.ds(pl.multiple_of(m * tile, tile), tile)
+        below = pl.ds(pl.multiple_of(row_count + m * tile, tile), tile)
+        real = jnp.dot(table_ref[rows, :], left[...], preferred_element_type=F32)
+        imag = jnp.dot(table_ref[below, :], left[...], preferred_element_type=F32)
+        for q in range(2):
+            lanes = slice(q * share, (q + 1) * share)
+            a, b = real[:, lanes], imag[:, lanes]
+            hr, hi = h_ref[0, 0, q, rows, :].astype(F32), h_ref[0, 1, q, rows, :].astype(F32)
+            right[rows, lanes] = (a * hr - b * hi).astype(BF16)
+            right[below, lanes] = (-(a * hi + b * hr)).astype(BF16)
+
+    @pl.loop(0, row_count // tile)
+    def _(m):
+        rows = pl.ds(pl.multiple_of(m * tile, tile), tile)
+        below = pl.ds(pl.multiple_of(row_count + m * tile, tile), tile)
+        real = jnp.dot(table_ref[rows, :], right[...], preferred_element_type=F32)
+        imag = jnp.dot(table_ref[below, :], right[...], preferred_element_type=F32)
+        turned = []
+        for q in range(2):
+            lanes = slice(q * share, (q + 1) * share)
+            a, b = real[:, lanes], imag[:, lanes]
+            ct, st = ct_ref[q, rows, :], st_ref[q, rows, :]
+            turned.append((a * ct + b * st, a * st - b * ct))
+        for p in range(blocks):
+            total = acc[p, rows, :]
+            for q in range(2):
+                total = total + cos_ref[2 * step + q, p] * turned[q][0]
+                total = total - sin_ref[2 * step + q, p] * turned[q][1]
+            acc[p, rows, :] = total
+
+    @pl.when(step == pl.num_programs(0) - 1)
+    def _():
+        scale = 1.0 / (2 * blocks * row_count)
+        out_ref[...] = (acc[...] * scale).astype(BF16)
+
+
+def call_long_filter(cos_block, sin_block, columns, cos_twist, sin_twist, response, table):
+    blocks, row_count, share = columns.shape
+    whole = lambda *shape: pl.BlockSpec(shape, lambda k: (0,) * len(shape))
+    twist = pl.BlockSpec((2, row_count, share), lambda k: (k, 0, 0))
+    flops = 2 * blocks * 2 * (2 * row_count) ** 2 * (2 * share)
+    return pl.pallas_call(
+        long_filter,
+        grid=(blocks,),
+        out_shape=jax.ShapeDtypeStruct(columns.shape, BF16),
+        in_specs=[
+            pl.BlockSpec(memory_space=pltpu.SMEM),
+            pl.BlockSpec(memory_space=pltpu.SMEM),
+            whole(blocks, row_count, share),
+            twist,
+            twist,
+            pl.BlockSpec((1, 2, 2, row_count, share), lambda k: (k, 0, 0, 0, 0)),
+            whole(2 * row_count, 2 * row_count),
+        ],
+        out_specs=whole(blocks, row_count, share),
+        scratch_shapes=[
+            pltpu.VMEM((blocks, row_count, share), F32),
+            pltpu.VMEM((2 * row_count, 2 * share), BF16),
+            pltpu.VMEM((2 * row_count, 2 * share), BF16),
+        ],
+        compiler_params=pltpu.CompilerParams(vmem_limit_bytes=56 * 2**20),
+        cost_estimate=pl.CostEstimate(flops=flops, bytes_accessed=40 * 2**20, transcendentals=0),
+    )(cos_block, sin_block, columns, cos_twist, sin_twist, response, table)
+
+
 def on_device(tokens, w_in, w_short, skip_gain, filter_spectra, w_out):
     row_count = tokens.shape[0]
     channels = w_in.shape[2]
@@ -57,6 +151,8 @@
     pieces = spread_filter(filter_spectra, seq_pos, seq_count)
 
     gathered = lax.all_gather(tokens, "ch", axis=1, tiled=True)
+    early = 1 + (seq_count - 1) * 4 // 7
+    gathered, pieces[1:early] = lax.optimization_barrier((gathered, pieces[1:early]))
     projected = [
         jnp.dot(gathered, w_in[:, s], preferred_element_type=F32).astype(BF16) for s in range(3)
     ]
@@ -68,6 +164,7 @@
         return taps[0] * extended[2:] + taps[1] * extended[1:-1] + taps[2] * extended[:-2]
 
     signal = (stream(0) * stream(2)).astype(BF16)
+    signal, pieces[early:] = lax.optimization_barrier((signal, pieces[early:]))
     second_gate = stream(1)
 
     columns = lax.all_to_all(
@@ -80,38 +177,19 @@
     senders = (seq_pos - jnp.arange(seq_count, dtype=jnp.int32)) % seq_count
     classes = (senders[:, None] * 2 + jnp.arange(2, dtype=jnp.int32)[None, :]).reshape(-1)
     cos_block, sin_block = phases(classes, jnp.arange(seq_count, dtype=jnp.int32), bin_count)
-    cos_twist, sin_twist = phases(jnp.arange(row_count, dtype=jnp.int32), classes, fft_length)
-    cos_twist, sin_twist = cos_twist[:, :, None], sin_twist[:, :, None]
-    table = jnp.asarray(dense_transform(row_count))
-
-    real = jnp.einsum("kp,pbc->bkc", cos_block.astype(BF16), columns, preferred_element_type=F32)
-    imag = -jnp.einsum("kp,pbc->bkc", sin_block.astype(BF16), columns, preferred_element_type=F32)
-    real, imag = (
-        real * cos_twist + imag * sin_twist,
-        imag * cos_twist - real * sin_twist,
-    )
-    packed = jnp.concatenate([real.astype(BF16), imag.astype(BF16)], 0)
-    packed = packed.reshape(2 * row_count, bin_count * share)
-    spectrum = jnp.dot(table, packed, preferred_element_type=F32).astype(BF16)
-    spectrum = spectrum.reshape(2, row_count, bin_count, share).astype(F32)
-
-    response = jnp.concatenate(pieces, 1).transpose(0, 2, 1, 3).astype(F32)
-    real = spectrum[0] * response[0] - spectrum[1] * response[1]
-    imag = spectrum[0] * response[1] + spectrum[1] * response[0]
-    packed = jnp.concatenate([real.astype(BF16), imag.astype(BF16)], 0)
-    packed = packed.reshape(2 * row_count, bin_count * share)
-    partial = lax.dot_general(
-        table, packed, (((0,), (0,)), ((), ())), preferred_element_type=F32
-    ).astype(BF16)
-    partial = partial.reshape(2, row_count, bin_count, share).astype(F32)
-    scale = 1.0 / fft_length
-    real = ((partial[0] * cos_twist - partial[1] * sin_twist) * scale).astype(BF16)
-    imag = ((partial[1] * cos_twist + partial[0] * sin_twist) * scale).astype(BF16)
-    convolved = jnp.einsum(
-        "kp,bkc->pbc", cos_block.astype(BF16), real, preferred_element_type=F32
-    ) - jnp.einsum("kp,bkc->pbc", sin_block.astype(BF16), imag, preferred_element_type=F32)
+    cos_twist, sin_twist = phases(classes, jnp.arange(row_count, dtype=jnp.int32), fft_length)
+    twist_shape = (bin_count, row_count, share)
+    convolved = call_long_filter(
+        cos_block,
+        sin_block,
+        columns,
+        jnp.broadcast_to(cos_twist[:, :, None], twist_shape),
+        jnp.broadcast_to(sin_twist[:, :, None], twist_shape),
+        jnp.stack(pieces),
+        jnp.asarray(dense_transform(row_count)),
+    )
     convolved = lax.all_to_all(
-        convolved.astype(BF16), "seq", split_axis=0, concat_axis=0, tiled=True
+        convolved, "seq", split_axis=0, concat_axis=0, tiled=True
     )
     convolved = convolved.transpose(1, 0, 2).reshape(row_count, channels).astype(F32)
 

time: 733 us -> 560 us (0.76); the launches traced: 723 us -> 559 us
  matrix products: 145 us -> 57.8 us
  waiting for transfers between devices: 325 us -> 250 us
  Pallas kernels: 0 us -> 71.5 us
  local copies, waits for them, and re-layouts: 85.5 us -> 44.9 us
  other arithmetic: 51.3 us -> 12.7 us
    all_gather x1, waiting for transfers between devices: 92.3 us -> 0.01 us  [on_device(): gathered = lax.all_gather(tokens, 'ch', axis=1, tiled=True)]
    dot_general x7 -> x0, matrix products: 86.2 us -> none  [the longest x2 32.4 us: on_device(): lax.dot_general(table, packed, (((0,), (0,)), ((), ())), preferred_elemen...]
    pallas_call x0 -> x1, Pallas kernels: none -> 71.5 us  [call_long_filter(): pl.pallas_call(long_filter, grid=(blocks,), out_shape=jax.ShapeDtypeStruc...]
    all_to_all x1, starting transfers between devices: 66.8 us -> 3.6 us  [on_device(): lax.all_to_all(convolved, 'seq', split_axis=0, concat_axis=0, tiled=True)]
    all_to_all x1, starting transfers between devices: 7.56 us -> 48 us  [on_device(): lax.all_to_all(signal.reshape(row_count, seq_count, share).transpose(1, 0...]
    all_to_all x1, waiting for transfers between devices: 0.01 us -> 33 us  [on_device(): lax.all_to_all(signal.reshape(row_count, seq_count, share).transpose(1, 0...]
    ppermute x1, starting transfers between devices: 1.74 us -> 24.4 us  [shifted(): return lax.ppermute(array, axis, pairs)]
    convert_element_type x2 -> x1, other arithmetic: 24.7 us -> 2.3 us  [on_device(): convolved.transpose(1, 0, 2).reshape(row_count, channels).astype(F32)]
  transfers between devices with their start and end apart: 12 -> 12, of which waited for: 7 -> 6; matrix products, arithmetic and copies ran while one was open for 8% -> 12% of each run, Pallas kernels for 0% -> 0%
where the time goes in v2:
time: 560 us; the launch traced here: 559 us
  waiting for transfers between devices  250 us (45%)
  starting transfers between devices  109 us (19%)
  Pallas kernels  71.5 us (13%)
  matrix products  57.8 us (10%)
  local copies, waits for them, and re-layouts  44.9 us (8%)
  between operations  13.7 us (2%)
  other arithmetic  12.7 us (2%)
    reduce_scatter x1, waiting for transfers between devices, on_device(): lax.psum_scatter(jnp.dot(gated_out, w_out, preferred_element_type=F32).as...  85.4 us
    ppermute x7, waiting for transfers between devices, spread_filter(): piece = lax.ppermute(piece, 'seq', pairs)  85.3 us
    pallas_call x1, Pallas kernels, call_long_filter(): pl.pallas_call(long_filter, grid=(blocks,), out_shape=jax.ShapeDtypeStruc...  71.5 us
    all_to_all x1, starting transfers between devices, on_device(): lax.all_to_all(signal.reshape(row_count, seq_count, share).transpose(1, 0...  48 us
    all_to_all x1, waiting for transfers between devices, on_device(): lax.all_to_all(convolved, 'seq', split_axis=0, concat_axis=0, tiled=True)  44.5 us
    dot_general x3, matrix products, on_device(): jnp.dot(gathered, w_in[:, s], preferred_element_type=F32).astype(BF16)  36.9 us
    all_to_all x1, waiting for transfers between devices, on_device(): lax.all_to_all(signal.reshape(row_count, seq_count, share).transpose(1, 0...  33 us
    ppermute x7, starting transfers between devices, spread_filter(): piece = lax.ppermute(piece, 'seq', pairs)  32.8 us
  transfers between devices with their start and end apart: 12, of which 6 were waited for; matrix products, arithmetic and copies ran while one was open for 12% of the time, Pallas kernels for 0%

profile of v2, /device:TPU:0, one launch (start us, length us, event | category | flops | bytes accessed | tf_op | source)
XLA Modules:
  0.0 559.2 jit_solution(2698731326826895088)
XLA Ops:
  6.5 0.7 all-gather.2.cloned.1.call-update
  7.4 3.7 constant_dynamic-slice_fusion
  11.1 0.5 collective-permute-start
  11.6 2.6 collective-permute-start.1
  14.2 2.5 collective-permute-start.2
  16.8 1.2 collective-permute-start.3
  18.0 1.2 collective-permute-start.5
  19.2 19.4 %collective-permute-done = bf16[2,2,1024,128]{3,2,1,0:T(8,128)(2,1)S(1)} collective-permute-done((bf16[2,2,1024,128]{3,2,1,0:T(8,128)(2,1)S(1)}, bf16[2,2,1024,128]{3,2,1,0:T(8,128)(2,1)S(1)}, u32[]{:S(2)}, u32[]{:S(2)}) %collective-permute-start) | collective-permute-done | bytes 1048608 | tf_op jit(solution)/shard_map/ppermute | solution.py:45
  38.6 2.4 collective-permute-start.6
  41.1 22.3 %collective-permute-start.7 = (bf16[2,2,1024,128]{3,2,1,0:T(8,128)(2,1)S(1)}, bf16[2,2,1024,128]{3,2,1,0:T(8,128)(2,1)}, u32[]{:S(2)}, u32[]{:S(2)}) collective-permute-start(bf16[2,2,1024,128]{3,2,1,0:T(8,128)(2,1)S(1)} %get-tuple-element.23), channel_id=1, source_target_pairs={{0,28},{4,0},{8,4},{12,8},{16,12},{20,16},{24,20},{28,24},{1,29},{... | collective-permute-start | bytes 3145736 | tf_op jit(solution)/shard_map/ppermute | solution.py:45
  63.4 65.8 %collective-permute-done.2 = bf16[2,2,1024,128]{3,2,1,0:T(8,128)(2,1)S(1)} collective-permute-done((bf16[2,2,1024,128]{3,2,1,0:T(8,128)(2,1)S(1)}, bf16[2,2,1024,128]{3,2,1,0:T(8,128)(2,1)S(1)}, u32[]{:S(2)}, u32[]{:S(2)}) %collective-permute-start.2) | collective-permute-done | bytes 1048608 | tf_op jit(solution)/shard_map/ppermute | solution.py:45
  129.2 1.0 copy-done.7
  130.2 13.8 %fusion.27 = bf16[1024,1024]{1,0:T(8,128)(2,1)S(1)} fusion(bf16[1024,4096]{1,0:T(8,128)(2,1)} %all-gather.2.cloned.1.call-done, bf16[4096,3,1024]{2,0,1:T(8,128)(2,1)} %param.8), kind=kOutput, calls=%fused_computation.38 | convolution fusion | flops 8590983168 | bytes 18874368 | tf_op jit(solution)/shard_map/dot_general | solution.py:157
  144.0 11.9 %fusion.30 = bf16[1024,1024]{1,0:T(8,128)(2,1)S(1)} fusion(bf16[1024,4096]{1,0:T(8,128)(2,1)S(1)} %copy-done.10, bf16[4096,3,1024]{2,0,1:T(8,128)(2,1)} %param.8), kind=kOutput, calls=%fused_computation.39 | convolution fusion | flops 8590983168 | bytes 18874368 | tf_op jit(solution)/shard_map/dot_general | solution.py:157
  156.0 11.2 %fusion.24 = bf16[1024,1024]{1,0:T(8,128)(2,1)S(1)} fusion(bf16[1024,4096]{1,0:T(8,128)(2,1)S(1)} %copy-done.10, bf16[4096,3,1024]{2,0,1:T(8,128)(2,1)} %param.8), kind=kOutput, calls=%fused_computation.37 | convolution fusion | flops 8590983168 | bytes 18874368 | tf_op jit(solution)/shard_map/dot_general | solution.py:157
  167.2 24.4 %collective-permute-start.4 = (bf16[3,2,1024]{2,1,0:T(2,128)(2,1)S(1)}, bf16[3,2,1024]{2,1,0:T(2,128)(2,1)S(1)}, u32[]{:S(2)}, u32[]{:S(2)}) collective-permute-start(bf16[3,2,1024]{2,1,0:T(2,128)(2,1)S(1)} %pad_maximum_fusion), channel_id=1, source_target_pairs={{0,4},{4,8},{8,12},{12,16},{16,20},{20,24},{24,28},{1,5},{5,9},{9,... | collective-permute-start | bytes 36872 | tf_op jit(solution)/shard_map/ppermute | solution.py:20
  191.7 0.6 collective-permute-done.4
  192.3 0.6 maximum_convert_fusion.1
  192.9 0.6 maximum_convert_fusion.2
  193.5 3.7 fusion.11
  197.3 2.9 copy.8
  200.2 2.4 copy.9
  202.6 48.0 %all-to-all-start = ((bf16[8,1024,128]{2,1,0:T(8,128)(2,1)}), bf16[8,1024,128]{2,1,0:T(8,128)(2,1)S(1)}, u32[]{:S(2)}, u32[]{:S(2)}) async-start(bf16[8,1024,128]{2,1,0:T(8,128)(2,1)} %bitcast.19), calls=%async_computation | async-start | bytes 4194304 | tf_op jit(solution)/shard_map/all_to_all | solution.py:170
  250.6 0.1 iota_add_fusion
  250.6 0.1 add.160
  250.7 2.4 bitcast_dynamic-update-slice_fusion.7
  253.1 0.7 fusion.47
  253.9 0.3 fusion.39
  254.2 1.0 bitcast_dynamic-update-slice_fusion.6
  255.3 1.1 bitcast_dynamic-update-slice_fusion.5
  256.3 1.0 bitcast_dynamic-update-slice_fusion.4
  257.4 2.3 bitcast_dynamic-update-slice_fusion.3
  259.7 2.3 bitcast_dynamic-update-slice_fusion.2
  262.0 2.2 bitcast_dynamic-update-slice_fusion.1
  264.2 2.4 bitcast_dynamic-update-slice_fusion.h_ref
  266.6 33.0 %all-to-all-done.x_ref = bf16[8,1024,128]{2,1,0:T(8,128)(2,1)S(1)} async-done(((bf16[8,1024,128]{2,1,0:T(8,128)(2,1)}), bf16[8,1024,128]{2,1,0:T(8,128)(2,1)S(1)}, u32[]{:S(2)}, u32[]{:S(2)}) %all-to-all-start) | async-done | bytes 2097184 | tf_op jit(solution)/shard_map/all_to_all | solution.py:170
  299.6 4.6 broadcast_in_dim.4.ct_ref
  304.2 4.6 broadcast_in_dim.5.st_ref
  308.8 71.5 %shard_map.73 = bf16[8,1024,128]{2,1,0:T(8,128)(2,1)} custom-call(f32[16,8]{1,0:T(8,128)} %get-tuple-element.45.cos_ref, f32[16,8]{1,0:T(8,128)} %get-tuple-element.44.sin_ref, bf16[8,1024,128]{2,1,0:T(8,128)(2,1)} %copy-done.2, f32[16,1024,128]{2,1,0:T(8,128)} %broadcast_in_dim.4.ct_ref, f32[16,1024,128]{2,1,0:T(8,128)} %broadcast_in_dim.5.st_ref, ...), custom_call_target="tpu_custom_call" | custom-call | flops 34359738368 | bytes 41943040 | tf_op jit(solution)/shard_map/pallas_call | solution.py:118
  380.3 3.6 all-to-all-start.1
  383.9 0.3 reduce-scatter.2.cloned.1.call-start
  384.2 4.2 maximum_convert_fusion
  388.4 44.5 %all-to-all-done.1 = bf16[8,1024,128]{2,1,0:T(8,128)(2,1)S(1)} async-done(((bf16[8,1024,128]{2,1,0:T(8,128)(2,1)}), bf16[8,1024,128]{2,1,0:T(8,128)(2,1)S(1)}, u32[]{:S(2)}, u32[]{:S(2)}) %all-to-all-start.1) | async-done | bytes 2097184 | tf_op jit(solution)/shard_map/all_to_all | solution.py:191
  432.9 2.3 convert_bitcast_fusion
  435.2 5.3 copy.10
  440.5 5.5 copy.11
  446.0 20.9 %convolution_convert_fusion = bf16[1024,4096]{1,0:T(8,128)(2,1)} fusion(bf16[1024,4096]{1,0:T(8,128)(2,1)} %param.12, f32[1026,1024]{1,0:T(8,128)} %maximum_convert_fusion, f32[1024,1024]{1,0:T(8,128)} %copy.11, bf16[1024,1024]{1,0:T(8,128)(2,1)S(1)} %copy-done, f32[1024]{0:T(1024)S(1)} %copy-done.11, f32[1024]{0:T(1024)S(1)} %bitcast.70, ...), kind=kOutput, calls=%fused_computation.9 | convolution fusion | flops 8604614656 | bytes 35667968 | tf_op jit(solution)/shard_map/dot_general | solution.py:199
  467.0 85.4 %reduce-scatter.2.cloned.1.call-done = bf16[256,4096]{1,0:T(8,128)(2,1)} async-done(((bf16[1024,4096]{1,0:T(8,128)(2,1)}), bf16[256,4096]{1,0:T(8,128)(2,1)}) %reduce-scatter.2.cloned.1.call-update) | async-done | bytes 2097168 | tf_op jit(solution)/shard_map/reduce_scatter | solution.py:198
  (37 shorter events, 0.2 us)
Async XLA Ops:
  6.5 123.6 %all-gather.2.cloned.1.call-start = ((), (), s32[]{:S(2)}) async-start(), calls=%async_computation.3 | async-start | bytes 10485760 | tf_op jit(solution)/shard_map/all_gather | solution.py:153
  11.1 27.5 %collective-permute-start = (bf16[2,2,1024,128]{3,2,1,0:T(8,128)(2,1)S(1)}, bf16[2,2,1024,128]{3,2,1,0:T(8,128)(2,1)S(1)}, u32[]{:S(2)}, u32[]{:S(2)}) collective-permute-start(bf16[2,2,1024,128]{3,2,1,0:T(8,128)(2,1)S(1)} %get-tuple-element.29), channel_id=1, source_target_pairs={{0,4},{4,8},{8,12},{12,16},{16,20},{20,24},{24,28},{28,0},{1,5},{5... | collective-permute-start | bytes 3145736 | tf_op jit(solution)/shard_map/ppermute | solution.py:45
  11.6 29.5 %collective-permute-start.1 = (bf16[2,2,1024,128]{3,2,1,0:T(8,128)(2,1)S(1)}, bf16[2,2,1024,128]{3,2,1,0:T(8,128)(2,1)S(1)}, u32[]{:S(2)}, u32[]{:S(2)}) collective-permute-start(bf16[2,2,1024,128]{3,2,1,0:T(8,128)(2,1)S(1)} %get-tuple-element.28), channel_id=1, source_target_pairs={{0,8},{4,12},{8,16},{12,20},{16,24},{20,28},{24,0},{28,4},{1,9},{5... | collective-permute-start | bytes 3145736 | tf_op jit(solution)/shard_map/ppermute | solution.py:45
  14.2 114.9 %collective-permute-start.2 = (bf16[2,2,1024,128]{3,2,1,0:T(8,128)(2,1)S(1)}, bf16[2,2,1024,128]{3,2,1,0:T(8,128)(2,1)S(1)}, u32[]{:S(2)}, u32[]{:S(2)}) collective-permute-start(bf16[2,2,1024,128]{3,2,1,0:T(8,128)(2,1)S(1)} %get-tuple-element.27), channel_id=1, source_target_pairs={{0,12},{4,16},{8,20},{12,24},{16,28},{20,0},{24,4},{28,8},{1,13},{... | collective-permute-start | bytes 3145736 | tf_op jit(solution)/shard_map/ppermute | solution.py:45
  16.8 113.4 %collective-permute-start.3 = (bf16[2,2,1024,128]{3,2,1,0:T(8,128)(2,1)S(1)}, bf16[2,2,1024,128]{3,2,1,0:T(8,128)(2,1)}, u32[]{:S(2)}, u32[]{:S(2)}) collective-permute-start(bf16[2,2,1024,128]{3,2,1,0:T(8,128)(2,1)S(1)} %get-tuple-element.26), channel_id=1, source_target_pairs={{0,16},{4,20},{8,24},{12,28},{16,0},{20,4},{24,8},{28,12},{1,17},{... | collective-permute-start | bytes 3145736 | tf_op jit(solution)/shard_map/ppermute | solution.py:45
  18.0 179.3 %collective-permute-start.5 = (bf16[2,2,1024,128]{3,2,1,0:T(8,128)(2,1)S(1)}, bf16[2,2,1024,128]{3,2,1,0:T(8,128)(2,1)}, u32[]{:S(2)}, u32[]{:S(2)}) collective-permute-start(bf16[2,2,1024,128]{3,2,1,0:T(8,128)(2,1)S(1)} %get-tuple-element.25), channel_id=1, source_target_pairs={{0,20},{4,24},{8,28},{12,0},{16,4},{20,8},{24,12},{28,16},{1,21},{... | collective-permute-start | bytes 3145736 | tf_op jit(solution)/shard_map/ppermute | solution.py:45
  38.6 90.5 %copy-start.3 = (bf16[2,2,1024,128]{3,2,1,0:T(8,128)(2,1)}, bf16[2,2,1024,128]{3,2,1,0:T(8,128)(2,1)S(1)}, u32[]{:S(2)}) copy-start(bf16[2,2,1024,128]{3,2,1,0:T(8,128)(2,1)S(1)} %collective-permute-done) | copy-start | bytes 3145732
  38.6 158.6 %collective-permute-start.6 = (bf16[2,2,1024,128]{3,2,1,0:T(8,128)(2,1)S(1)}, bf16[2,2,1024,128]{3,2,1,0:T(8,128)(2,1)}, u32[]{:S(2)}, u32[]{:S(2)}) collective-permute-start(bf16[2,2,1024,128]{3,2,1,0:T(8,128)(2,1)S(1)} %get-tuple-element.24), channel_id=1, source_target_pairs={{0,24},{4,28},{8,0},{12,4},{16,8},{20,12},{24,16},{28,20},{1,25},{... | collective-permute-start | bytes 3145736 | tf_op jit(solution)/shard_map/ppermute | solution.py:45
  41.1 88.1 %copy-start.5 = (bf16[2,2,1024,128]{3,2,1,0:T(8,128)(2,1)}, bf16[2,2,1024,128]{3,2,1,0:T(8,128)(2,1)S(1)}, u32[]{:S(2)}) copy-start(bf16[2,2,1024,128]{3,2,1,0:T(8,128)(2,1)S(1)} %collective-permute-done.1) | copy-start | bytes 3145732
  41.1 156.2 %collective-permute-start.7 = (bf16[2,2,1024,128]{3,2,1,0:T(8,128)(2,1)S(1)}, bf16[2,2,1024,128]{3,2,1,0:T(8,128)(2,1)}, u32[]{:S(2)}, u32[]{:S(2)}) collective-permute-start(bf16[2,2,1024,128]{3,2,1,0:T(8,128)(2,1)S(1)} %get-tuple-element.23), channel_id=1, source_target_pairs={{0,28},{4,0},{8,4},{12,8},{16,12},{20,16},{24,20},{28,24},{1,29},{... | collective-permute-start | bytes 3145736 | tf_op jit(solution)/shard_map/ppermute | solution.py:45
  129.2 1.0 copy-start.7
  130.2 13.8 %copy-start.10 = (bf16[1024,4096]{1,0:T(8,128)(2,1)S(1)}, bf16[1024,4096]{1,0:T(8,128)(2,1)}, u32[]{:S(2)}) copy-start(bf16[1024,4096]{1,0:T(8,128)(2,1)} %all-gather.2.cloned.1.call-done) | copy-start | bytes 25165828
  144.0 23.2 %copy-start.1 = (bf16[1024,1024]{1,0:T(8,128)(2,1)}, bf16[1024,1024]{1,0:T(8,128)(2,1)S(1)}, u32[]{:S(2)}) copy-start(bf16[1024,1024]{1,0:T(8,128)(2,1)S(1)} %fusion.27) | copy-start | bytes 6291460
  155.9 35.7 %copy-start.9 = (f32[3,3,1024]{2,1,0:T(4,128)S(1)}, f32[3,3,1024]{2,1,0:T(4,128)}, u32[]{:S(2)}) copy-start(f32[3,3,1024]{2,1,0:T(4,128)} %param.9) | copy-start | bytes 110596
  167.2 25.0 %collective-permute-start.4 = (bf16[3,2,1024]{2,1,0:T(2,128)(2,1)S(1)}, bf16[3,2,1024]{2,1,0:T(2,128)(2,1)S(1)}, u32[]{:S(2)}, u32[]{:S(2)}) collective-permute-start(bf16[3,2,1024]{2,1,0:T(2,128)(2,1)S(1)} %pad_maximum_fusion), channel_id=1, source_target_pairs={{0,4},{4,8},{8,12},{12,16},{16,20},{20,24},{24,28},{1,5},{5,9},{9,... | collective-permute-start | bytes 36872 | tf_op jit(solution)/shard_map/ppermute | solution.py:20
  202.6 51.7 %copy-start.4 = (bf16[2,2,1024,128]{3,2,1,0:T(8,128)(2,1)S(1)}, bf16[2,2,1024,128]{3,2,1,0:T(8,128)(2,1)}, u32[]{:S(2)}) copy-start(bf16[2,2,1024,128]{3,2,1,0:T(8,128)(2,1)} %copy-done.3) | copy-start | bytes 3145732
  202.6 97.1 %all-to-all-start = ((bf16[8,1024,128]{2,1,0:T(8,128)(2,1)}), bf16[8,1024,128]{2,1,0:T(8,128)(2,1)S(1)}, u32[]{:S(2)}, u32[]{:S(2)}) async-start(bf16[8,1024,128]{2,1,0:T(8,128)(2,1)} %bitcast.19), calls=%async_computation | async-start | bytes 4194304 | tf_op jit(solution)/shard_map/all_to_all | solution.py:170
  250.7 4.5 copy-start.6
  250.7 5.6 %copy-start.8 = (bf16[2,2,1024,128]{3,2,1,0:T(8,128)(2,1)S(1)}, bf16[2,2,1024,128]{3,2,1,0:T(8,128)(2,1)}, u32[]{:S(2)}) copy-start(bf16[2,2,1024,128]{3,2,1,0:T(8,128)(2,1)} %copy-done.7) | copy-start | bytes 3145732
  299.6 4.6 copy-start.2
  380.3 52.6 %all-to-all-start.1 = ((bf16[8,1024,128]{2,1,0:T(8,128)(2,1)}), bf16[8,1024,128]{2,1,0:T(8,128)(2,1)S(1)}, u32[]{:S(2)}, u32[]{:S(2)}) async-start(bf16[8,1024,128]{2,1,0:T(8,128)(2,1)} %shard_map.73), calls=%async_computation.1 | async-start | bytes 4194304 | tf_op jit(solution)/shard_map/all_to_all | solution.py:191
  383.9 168.5 %reduce-scatter.2.cloned.1.call-start = ((), (), s32[]{:S(2)}) async-start(), calls=%async_computation.4 | async-start | bytes 10485760 | tf_op jit(solution)/shard_map/reduce_scatter | solution.py:198
  440.5 5.5 copy-start
  440.5 5.5 copy-start.11
Sparse Core Ops, SparseCore 0:
  9.2 90.2 all-gather.1
  467.1 85.2 reduce-scatter.1

commit v3 on v2

--- a/solution.py
+++ b/solution.py
@@ -33,21 +33,16 @@
     return jnp.cos(angle), jnp.sin(angle)
 
 
-def spread_filter(filter_spectra, seq_pos, seq_count):
-    _, own, row_count, channels = filter_spectra.shape
-    share = channels // seq_count
-    pieces = []
-    for k in range(seq_count):
-        first = (seq_pos + k) % seq_count * share
-        piece = lax.dynamic_slice_in_dim(filter_spectra, first, share, 3)
-        if k:
-            pairs = [(s, (s + k) % seq_count) for s in range(seq_count)]
-            piece = lax.ppermute(piece, "seq", pairs)
-        pieces.append(piece)
-    return pieces
-
-
-def long_filter(cos_ref, sin_ref, x_ref, ct_ref, st_ref, h_ref, table_ref, out_ref, acc, left, right):
+def spread_filter(filter_spectra, own):
+    _, _, row_count, channels = filter_spectra.shape
+    seq_count = lax.axis_size("seq")
+    pieces = filter_spectra[:, own].reshape(2, row_count, seq_count, channels // seq_count)
+    return lax.all_to_all(
+        pieces.transpose(2, 0, 1, 3), "seq", split_axis=0, concat_axis=0, tiled=True
+    )
+
+
+def long_filter(cos_ref, sin_ref, x_ref, ct_ref, st_ref, h0_ref, h1_ref, table_ref, out_ref, acc, left, right):
     blocks, row_count, share = x_ref.shape
     step = pl.program_id(0)
     chunk, tile = 64, 512
@@ -81,7 +76,8 @@
         for q in range(2):
             lanes = slice(q * share, (q + 1) * share)
             a, b = real[:, lanes], imag[:, lanes]
-            hr, hi = h_ref[0, 0, q, rows, :].astype(F32), h_ref[0, 1, q, rows, :].astype(F32)
+            h_ref = (h0_ref, h1_ref)[q]
+            hr, hi = h_ref[0, 0, rows, :].astype(F32), h_ref[0, 1, rows, :].astype(F32)
             right[rows, lanes] = (a * hr - b * hi).astype(BF16)
             right[below, lanes] = (-(a * hi + b * hr)).astype(BF16)
 
@@ -110,10 +106,11 @@
         out_ref[...] = (acc[...] * scale).astype(BF16)
 
 
-def call_long_filter(cos_block, sin_block, columns, cos_twist, sin_twist, response, table):
+def call_long_filter(cos_block, sin_block, columns, cos_twist, sin_twist, first, second, table):
     blocks, row_count, share = columns.shape
     whole = lambda *shape: pl.BlockSpec(shape, lambda k: (0,) * len(shape))
     twist = pl.BlockSpec((2, row_count, share), lambda k: (k, 0, 0))
+    piece = pl.BlockSpec((1, 2, row_count, share), lambda k: (k, 0, 0, 0))
     flops = 2 * blocks * 2 * (2 * row_count) ** 2 * (2 * share)
     return pl.pallas_call(
         long_filter,
@@ -125,7 +122,8 @@
             whole(blocks, row_count, share),
             twist,
             twist,
-            pl.BlockSpec((1, 2, 2, row_count, share), lambda k: (k, 0, 0, 0, 0)),
+            piece,
+            piece,
             whole(2 * row_count, 2 * row_count),
         ],
         out_specs=whole(blocks, row_count, share),
@@ -136,23 +134,21 @@
         ],
         compiler_params=pltpu.CompilerParams(vmem_limit_bytes=56 * 2**20),
         cost_estimate=pl.CostEstimate(flops=flops, bytes_accessed=40 * 2**20, transcendentals=0),
-    )(cos_block, sin_block, columns, cos_twist, sin_twist, response, table)
+    )(cos_block, sin_block, columns, cos_twist, sin_twist, first, second, table)
 
 
 def on_device(tokens, w_in, w_short, skip_gain, filter_spectra, w_out):
     row_count = tokens.shape[0]
     channels = w_in.shape[2]
     seq_count = lax.axis_size("seq")
-    seq_pos = lax.axis_index("seq")
     bin_count = 2 * seq_count
     share = channels // seq_count
     fft_length = bin_count * row_count
 
-    pieces = spread_filter(filter_spectra, seq_pos, seq_count)
-
+    first_filter = spread_filter(filter_spectra, 0)
     gathered = lax.all_gather(tokens, "ch", axis=1, tiled=True)
-    early = 1 + (seq_count - 1) * 4 // 7
-    gathered, pieces[1:early] = lax.optimization_barrier((gathered, pieces[1:early]))
+    gathered, first_filter = lax.optimization_barrier((gathered, first_filter))
+    second_filter = spread_filter(filter_spectra, 1)
     projected = [
         jnp.dot(gathered, w_in[:, s], preferred_element_type=F32).astype(BF16) for s in range(3)
     ]
@@ -164,7 +160,7 @@
         return taps[0] * extended[2:] + taps[1] * extended[1:-1] + taps[2] * extended[:-2]
 
     signal = (stream(0) * stream(2)).astype(BF16)
-    signal, pieces[early:] = lax.optimization_barrier((signal, pieces[early:]))
+    signal, second_filter = lax.optimization_barrier((signal, second_filter))
     second_gate = stream(1)
 
     columns = lax.all_to_all(
@@ -174,8 +170,7 @@
         concat_axis=0,
         tiled=True,
     )
-    senders = (seq_pos - jnp.arange(seq_count, dtype=jnp.int32)) % seq_count
-    classes = (senders[:, None] * 2 + jnp.arange(2, dtype=jnp.int32)[None, :]).reshape(-1)
+    classes = jnp.arange(bin_count, dtype=jnp.int32)
     cos_block, sin_block = phases(classes, jnp.arange(seq_count, dtype=jnp.int32), bin_count)
     cos_twist, sin_twist = phases(classes, jnp.arange(row_count, dtype=jnp.int32), fft_length)
     twist_shape = (bin_count, row_count, share)
@@ -185,22 +180,35 @@
         columns,
         jnp.broadcast_to(cos_twist[:, :, None], twist_shape),
         jnp.broadcast_to(sin_twist[:, :, None], twist_shape),
-        jnp.stack(pieces),
+        first_filter,
+        second_filter,
         jnp.asarray(dense_transform(row_count)),
     )
-    convolved = lax.all_to_all(
-        convolved, "seq", split_axis=0, concat_axis=0, tiled=True
-    )
-    convolved = convolved.transpose(1, 0, 2).reshape(row_count, channels).astype(F32)
-
-    response = convolved + skip_gain * signal.astype(F32)
-    gated_out = (second_gate * response).astype(BF16)
-    return lax.psum_scatter(
-        jnp.dot(gated_out, w_out, preferred_element_type=F32).astype(BF16),
-        "ch",
-        scatter_dimension=0,
-        tiled=True,
-    )
+    owners = lax.axis_size("ch")
+    half = row_count // (2 * owners)
+
+    def rows_of(array, h, axis):
+        shape = array.shape[:axis] + (owners, 2, half) + array.shape[axis + 1 :]
+        picked = lax.index_in_dim(array.reshape(shape), h, axis + 1, keepdims=False)
+        return picked.reshape(array.shape[:axis] + (owners * half,) + array.shape[axis + 1 :])
+
+    outs = []
+    for h in range(2):
+        back = lax.all_to_all(
+            rows_of(convolved, h, 1), "seq", split_axis=0, concat_axis=0, tiled=True
+        )
+        back = back.transpose(1, 0, 2).reshape(owners * half, channels).astype(F32)
+        response = back + skip_gain * rows_of(signal, h, 0).astype(F32)
+        gated_out = (rows_of(second_gate, h, 0) * response).astype(BF16)
+        outs.append(
+            lax.psum_scatter(
+                jnp.dot(gated_out, w_out, preferred_element_type=F32).astype(BF16),
+                "ch",
+                scatter_dimension=0,
+                tiled=True,
+            )
+        )
+    return jnp.concatenate(outs, 0)
 
 
 def solution(mesh):

time: 560 us -> 565 us (level)
  starting transfers between devices: 109 us -> 27.1 us
  waiting for transfers between devices: 250 us -> 308 us
  local copies, waits for them, and re-layouts: 44.9 us -> 68.2 us
  other arithmetic: 12.7 us -> 19.4 us
    all_to_all x1 -> x4, waiting for transfers between devices: 44.5 us -> 162 us  [the longest x2 131 us: spread_filter(): lax.all_to_all(pieces.transpose(2, 0, 1, 3), 'seq', split_axis=0, concat_...]
    ppermute x7 -> x0, waiting for transfers between devices: 85.3 us -> none  [spread_filter(): piece = lax.ppermute(piece, 'seq', pairs)]
    all_to_all x1, starting transfers between devices: 48 us -> 5.67 us  [on_device(): lax.all_to_all(signal.reshape(row_count, seq_count, share).transpose(1, 0...]
    ppermute x7 -> x0, starting transfers between devices: 32.8 us -> none  [spread_filter(): piece = lax.ppermute(piece, 'seq', pairs)]
    ppermute x1, starting transfers between devices: 24.4 us -> 2.44 us  [shifted(): return lax.ppermute(array, axis, pairs)]
    another operation x1 -> x6, local copies, waits for them, and re-layouts: 2.37 us -> 22.6 us  [the longest x2 13.1 us: spread_filter(): filter_spectra[:, own]]
    all_to_all x1 -> x4, starting transfers between devices: 3.6 us -> 18.7 us  [the longest x2 10.9 us: spread_filter(): lax.all_to_all(pieces.transpose(2, 0, 1, 3), 'seq', split_axis=0, concat_...]
    all_to_all x1, waiting for transfers between devices: 33 us -> 48 us  [on_device(): lax.all_to_all(signal.reshape(row_count, seq_count, share).transpose(1, 0...]
  transfers between devices with their start and end apart: 12 -> 9, of which waited for: 6 -> 8; matrix products, arithmetic and copies ran while one was open for 12% -> 19% of each run, Pallas kernels for 0% -> 0%
where the time goes in v3:
time: 565 us; the launch traced here: 563 us
  waiting for transfers between devices  308 us (55%)
  Pallas kernels  71.5 us (13%)
  local copies, waits for them, and re-layouts  68.2 us (12%)
  matrix products  56 us (10%)
  starting transfers between devices  27.1 us (5%)
  other arithmetic  19.4 us (3%)
  between operations  13.3 us (2%)
    all_to_all x2, waiting for transfers between devices, spread_filter(): lax.all_to_all(pieces.transpose(2, 0, 1, 3), 'seq', split_axis=0, concat_...  131 us
    reduce_scatter x2, waiting for transfers between devices, on_device(): lax.psum_scatter(jnp.dot(gated_out, w_out, preferred_element_type=F32).as...  96.9 us
    pallas_call x1, Pallas kernels, call_long_filter(): pl.pallas_call(long_filter, grid=(blocks,), out_shape=jax.ShapeDtypeStruc...  71.5 us
    all_to_all x1, waiting for transfers between devices, on_device(): lax.all_to_all(signal.reshape(row_count, seq_count, share).transpose(1, 0...  48 us
    dot_general x3, matrix products, on_device(): jnp.dot(gathered, w_in[:, s], preferred_element_type=F32).astype(BF16)  36.9 us
    all_to_all x2, waiting for transfers between devices, on_device(): lax.all_to_all(rows_of(convolved, h, 1), 'seq', split_axis=0, concat_axis...  30.6 us
    dot_general x2, matrix products, on_device(): jnp.dot(gated_out, w_out, preferred_element_type=F32).astype(BF16)  19 us
    unnamed x14, local copies, waits for them, and re-layouts  13.7 us
  transfers between devices with their start and end apart: 9, of which 8 were waited for; matrix products, arithmetic and copies ran while one was open for 19% of the time, Pallas kernels for 0%

profile of v3, /device:TPU:0, one launch (start us, length us, event | category | flops | bytes accessed | tf_op | source)
XLA Modules:
  0.0 563.5 jit_solution(12176927674815996621)
XLA Ops:
  6.5 0.7 all-gather.2.cloned.1.call-update
  7.3 5.9 %fusion.46 = (bf16[2,1,1024,1024]{3,2,1,0:T(8,128)(2,1)}, bf16[2,1,1024,1024]{3,2,1,0:T(8,128)(2,1)}) fusion(bf16[2,2,1024,1024]{3,2,1,0:T(8,128)(2,1)} %param.11), kind=kLoop, calls=%fused_computation.72 | loop fusion | bytes 16777216 | tf_op jit(solution)/shard_map/slice | solution.py:39
  13.2 6.2 %copy.26 = bf16[2,1,1024,1024]{2,3,0,1:T(8,128)(2,1)} copy(bf16[2,1,1024,1024]{3,2,1,0:T(8,128)(2,1)} %get-tuple-element.14) | data formatting | bytes 8388608
  19.4 6.7 %copy.9 = bf16[2,1024,8,128]{3,1,0,2:T(8,128)(2,1)} copy(bf16[2,1024,8,128]{1,3,2,0:T(8,128)(2,1)} %bitcast.81) | data formatting | bytes 8388608 | tf_op jit(solution)/shard_map/reshape;squeeze | solution.py:39
  26.1 6.4 %all-to-all-start = ((bf16[8,2,1024,128]{3,2,1,0:T(8,128)(2,1)}), bf16[8,2,1024,128]{3,2,1,0:T(8,128)(2,1)}, u32[]{:S(2)}, u32[]{:S(2)}) async-start(bf16[8,2,1024,128]{3,2,1,0:T(8,128)(2,1)} %bitcast.80), calls=%async_computation | async-start | bytes 8388608 | tf_op jit(solution)/shard_map/all_to_all | solution.py:40
  32.4 6.3 %copy.27 = bf16[2,1,1024,1024]{2,3,0,1:T(8,128)(2,1)} copy(bf16[2,1,1024,1024]{3,2,1,0:T(8,128)(2,1)} %get-tuple-element.13) | data formatting | bytes 8388608
  38.7 6.4 %copy.12 = bf16[2,1024,8,128]{3,1,0,2:T(8,128)(2,1)} copy(bf16[2,1024,8,128]{1,3,2,0:T(8,128)(2,1)} %bitcast.82) | data formatting | bytes 8388608 | tf_op jit(solution)/shard_map/reshape;squeeze | solution.py:39
  45.1 81.4 %all-to-all-done.h0_ref = bf16[8,2,1024,128]{3,2,1,0:T(8,128)(2,1)} async-done(((bf16[8,2,1024,128]{3,2,1,0:T(8,128)(2,1)}), bf16[8,2,1024,128]{3,2,1,0:T(8,128)(2,1)}, u32[]{:S(2)}, u32[]{:S(2)}) %all-to-all-start) | async-done | bytes 4194336 | tf_op jit(solution)/shard_map/all_to_all | solution.py:40
  126.5 4.6 all-to-all-start.1
  131.1 13.8 %fusion.21 = bf16[1024,1024]{1,0:T(8,128)(2,1)S(1)} fusion(bf16[1024,4096]{1,0:T(8,128)(2,1)} %all-gather.2.cloned.1.call-done, bf16[4096,3,1024]{2,0,1:T(8,128)(2,1)} %param.8), kind=kOutput, calls=%fused_computation.38 | convolution fusion | flops 8590983168 | bytes 18874368 | tf_op jit(solution)/shard_map/dot_general | solution.py:153
  145.0 11.2 %fusion.24 = bf16[1024,1024]{1,0:T(8,128)(2,1)S(1)} fusion(bf16[1024,4096]{1,0:T(8,128)(2,1)S(1)} %copy-done.5, bf16[4096,3,1024]{2,0,1:T(8,128)(2,1)} %param.8), kind=kOutput, calls=%fused_computation.39 | convolution fusion | flops 8590983168 | bytes 18874368 | tf_op jit(solution)/shard_map/dot_general | solution.py:153
  156.2 11.9 %fusion.27 = bf16[1024,1024]{1,0:T(8,128)(2,1)S(1)} fusion(bf16[1024,4096]{1,0:T(8,128)(2,1)S(1)} %copy-done.5, bf16[4096,3,1024]{2,0,1:T(8,128)(2,1)} %param.8), kind=kOutput, calls=%fused_computation.40 | convolution fusion | flops 8590983168 | bytes 18874368 | tf_op jit(solution)/shard_map/dot_general | solution.py:153
  168.2 2.4 collective-permute-start
  171.3 0.6 maximum_convert_fusion.1
  172.6 2.7 fusion.11
  175.3 49.8 %all-to-all-done.1.h1_ref = bf16[8,2,1024,128]{3,2,1,0:T(8,128)(2,1)} async-done(((bf16[8,2,1024,128]{3,2,1,0:T(8,128)(2,1)}), bf16[8,2,1024,128]{3,2,1,0:T(8,128)(2,1)}, u32[]{:S(2)}, u32[]{:S(2)}) %all-to-all-start.1) | async-done | bytes 4194336 | tf_op jit(solution)/shard_map/all_to_all | solution.py:40
  225.1 2.5 copy.13
  227.6 3.9 copy.14
  231.6 5.7 %all-to-all-start.2 = ((bf16[8,1024,128]{2,1,0:T(8,128)(2,1)}), bf16[8,1024,128]{2,1,0:T(8,128)(2,1)}, u32[]{:S(2)}, u32[]{:S(2)}) async-start(bf16[8,1024,128]{2,1,0:T(8,128)(2,1)} %bitcast.84), calls=%async_computation.2 | async-start | bytes 4194304 | tf_op jit(solution)/shard_map/all_to_all | solution.py:166
  237.2 0.7 fusion.44
  238.4 48.0 %all-to-all-done.2.x_ref = bf16[8,1024,128]{2,1,0:T(8,128)(2,1)} async-done(((bf16[8,1024,128]{2,1,0:T(8,128)(2,1)}), bf16[8,1024,128]{2,1,0:T(8,128)(2,1)}, u32[]{:S(2)}, u32[]{:S(2)}) %all-to-all-start.2) | async-done | bytes 2097184 | tf_op jit(solution)/shard_map/all_to_all | solution.py:166
  286.4 4.5 broadcast_in_dim.4.ct_ref
  290.9 4.4 broadcast_in_dim.5.st_ref
  295.4 71.5 %shard_map.73 = bf16[8,1024,128]{2,1,0:T(8,128)(2,1)} custom-call(f32[16,8]{1,0:T(8,128)} %get-tuple-element.38.cos_ref, f32[16,8]{1,0:T(8,128)} %get-tuple-element.37.sin_ref, bf16[8,1024,128]{2,1,0:T(8,128)(2,1)} %all-to-all-done.2.x_ref, f32[16,1024,128]{2,1,0:T(8,128)} %broadcast_in_dim.4.ct_ref, f32[16,1024,128]{2,1,0:T(8,128)} %broadcast_in_dim.5.st_ref, ...), custom_call_target="tpu_custom_call" | custom-call | flops 34359738368 | bytes 41943040 | tf_op jit(solution)/shard_map/pallas_call | solution.py:115
  366.8 2.8 fusion.48
  369.6 1.3 copy.21
  370.9 3.6 all-to-all-start.3
  374.5 1.6 fusion.49
  376.1 2.3 copy.24
  378.4 22.6 %all-to-all-done.3 = bf16[8,512,128]{1,2,0:T(8,128)(2,1)S(1)} async-done(((bf16[8,512,128]{1,2,0:T(8,128)(2,1)}), bf16[8,512,128]{1,2,0:T(8,128)(2,1)S(1)}, u32[]{:S(2)}, u32[]{:S(2)}) %all-to-all-start.3) | async-done | bytes 1048608 | tf_op jit(solution)/shard_map/all_to_all | solution.py:197
  401.0 4.2 all-to-all-start.4
  405.5 1.5 bitcast_convert_fusion.1
  407.0 1.9 copy.22
  408.9 1.5 bitcast_convert_fusion
  410.3 1.8 copy.25
  412.2 2.2 maximum_convert_fusion
  414.4 1.2 fusion.15
  415.6 2.4 fusion.47
  418.0 3.0 copy.20
  421.0 2.9 copy.23
  423.9 8.0 %all-to-all-done.4 = bf16[8,512,128]{1,2,0:T(8,128)(2,1)} async-done(((bf16[8,512,128]{1,2,0:T(8,128)(2,1)}), bf16[8,512,128]{1,2,0:T(8,128)(2,1)}, u32[]{:S(2)}, u32[]{:S(2)}) %all-to-all-start.4) | async-done | bytes 1048608 | tf_op jit(solution)/shard_map/all_to_all | solution.py:197
  431.9 4.8 fusion.20
  436.6 9.5 %convolution_convert_fusion.1 = bf16[512,4096]{1,0:T(8,128)(2,1)} fusion(bf16[512,1024]{0,1:T(8,128)(2,1)S(1)} %get-tuple-element.33, bf16[1024,4096]{1,0:T(8,128)(2,1)} %param.12), kind=kOutput, calls=%fused_computation.10 | convolution fusion | flops 4297064448 | bytes 13631488 | tf_op jit(solution)/shard_map/dot_general | solution.py:205
  446.2 1.1 copy-done.2
  447.3 9.6 %convolution_convert_fusion = bf16[512,4096]{1,0:T(8,128)(2,1)} fusion(bf16[512,1024]{0,1:T(8,128)(2,1)S(1)} %copy-done.2, bf16[1024,4096]{1,0:T(8,128)(2,1)} %param.12), kind=kOutput, calls=%fused_computation.9 | convolution fusion | flops 4297064448 | bytes 13631488 | tf_op jit(solution)/shard_map/dot_general | solution.py:205
  456.9 41.0 %reduce-scatter.3.cloned.1.call-done = bf16[128,4096]{1,0:T(8,128)(2,1)} async-done(((bf16[512,4096]{1,0:T(8,128)(2,1)}), bf16[128,4096]{1,0:T(8,128)(2,1)}) %reduce-scatter.3.cloned.1.call-update) | async-done | bytes 1048592 | tf_op jit(solution)/shard_map/reduce_scatter | solution.py:204
  497.9 56.0 %reduce-scatter.5.cloned.1.call-done = bf16[128,4096]{1,0:T(8,128)(2,1)} async-done(((bf16[512,4096]{1,0:T(8,128)(2,1)}), bf16[128,4096]{1,0:T(8,128)(2,1)}) %reduce-scatter.5.cloned.1.call-update) | async-done | bytes 1048592 | tf_op jit(solution)/shard_map/reduce_scatter | solution.py:204
  553.8 3.1 pad_maximum_fusion
  (26 shorter events, 2.2 us)
Async XLA Ops:
  6.5 124.6 %all-gather.2.cloned.1.call-start = ((), (), s32[]{:S(2)}) async-start(), calls=%async_computation.7 | async-start | bytes 10485760 | tf_op jit(solution)/shard_map/all_gather | solution.py:149
  26.1 100.5 %all-to-all-start = ((bf16[8,2,1024,128]{3,2,1,0:T(8,128)(2,1)}), bf16[8,2,1024,128]{3,2,1,0:T(8,128)(2,1)}, u32[]{:S(2)}, u32[]{:S(2)}) async-start(bf16[8,2,1024,128]{3,2,1,0:T(8,128)(2,1)} %bitcast.80), calls=%async_computation | async-start | bytes 8388608 | tf_op jit(solution)/shard_map/all_to_all | solution.py:40
  126.5 98.6 %all-to-all-start.1 = ((bf16[8,2,1024,128]{3,2,1,0:T(8,128)(2,1)}), bf16[8,2,1024,128]{3,2,1,0:T(8,128)(2,1)}, u32[]{:S(2)}, u32[]{:S(2)}) async-start(bf16[8,2,1024,128]{3,2,1,0:T(8,128)(2,1)} %bitcast.79), calls=%async_computation.1 | async-start | bytes 8388608 | tf_op jit(solution)/shard_map/all_to_all | solution.py:40
  131.1 13.8 %copy-start.5 = (bf16[1024,4096]{1,0:T(8,128)(2,1)S(1)}, bf16[1024,4096]{1,0:T(8,128)(2,1)}, u32[]{:S(2)}) copy-start(bf16[1024,4096]{1,0:T(8,128)(2,1)} %all-gather.2.cloned.1.call-done) | copy-start | bytes 25165828
  156.2 12.0 %copy-start.1 = (bf16[1024,1024]{1,0:T(8,128)(2,1)}, bf16[1024,1024]{1,0:T(8,128)(2,1)S(1)}, u32[]{:S(2)}) copy-start(bf16[1024,1024]{1,0:T(8,128)(2,1)S(1)} %fusion.24) | copy-start | bytes 6291460
  156.2 14.5 %copy-start.3 = (f32[3,3,1024]{2,1,0:T(4,128)S(1)}, f32[3,3,1024]{2,1,0:T(4,128)}, u32[]{:S(2)}) copy-start(f32[3,3,1024]{2,1,0:T(4,128)} %param.9) | copy-start | bytes 110596
  168.2 3.1 collective-permute-start
  231.6 54.8 %all-to-all-start.2 = ((bf16[8,1024,128]{2,1,0:T(8,128)(2,1)}), bf16[8,1024,128]{2,1,0:T(8,128)(2,1)}, u32[]{:S(2)}, u32[]{:S(2)}) async-start(bf16[8,1024,128]{2,1,0:T(8,128)(2,1)} %bitcast.84), calls=%async_computation.2 | async-start | bytes 4194304 | tf_op jit(solution)/shard_map/all_to_all | solution.py:166
  370.9 30.1 %all-to-all-start.3 = ((bf16[8,512,128]{1,2,0:T(8,128)(2,1)}), bf16[8,512,128]{1,2,0:T(8,128)(2,1)S(1)}, u32[]{:S(2)}, u32[]{:S(2)}) async-start(bf16[8,512,128]{1,2,0:T(8,128)(2,1)} %copy.21), calls=%async_computation.3 | async-start | bytes 2097152 | tf_op jit(solution)/shard_map/all_to_all | solution.py:197
  401.0 30.8 %all-to-all-start.4 = ((bf16[8,512,128]{1,2,0:T(8,128)(2,1)}), bf16[8,512,128]{1,2,0:T(8,128)(2,1)}, u32[]{:S(2)}, u32[]{:S(2)}) async-start(bf16[8,512,128]{1,2,0:T(8,128)(2,1)} %copy.24), calls=%async_computation.5 | async-start | bytes 2097152 | tf_op jit(solution)/shard_map/all_to_all | solution.py:197
  405.3 92.6 %reduce-scatter.3.cloned.1.call-start = ((), (), s32[]{:S(2)}) async-start(), calls=%async_computation.8 | async-start | bytes 5242880 | tf_op jit(solution)/shard_map/reduce_scatter | solution.py:204
  418.0 13.9 %copy-start = (f32[512,1024]{0,1:T(8,128)S(1)}, f32[512,1024]{0,1:T(8,128)}, u32[]{:S(2)}) copy-start(f32[512,1024]{0,1:T(8,128)} %copy.22) | copy-start | bytes 6291460
  418.0 13.9 %copy-start.4 = (f32[1024]{0:T(1024)S(1)}, f32[1024]{0:T(1024)}, u32[]{:S(2)}) copy-start(f32[1024]{0:T(1024)} %param.10) | copy-start | bytes 12292
  446.1 1.2 copy-start.2
  446.1 107.7 %reduce-scatter.5.cloned.1.call-start = ((), (), s32[]{:S(2)}) async-start(), calls=%async_computation.9 | async-start | bytes 5242880 | tf_op jit(solution)/shard_map/reduce_scatter | solution.py:204
Sparse Core Ops, SparseCore 0:
  9.2 90.2 all-gather.1
  446.3 51.5 reduce-scatter.2
  501.1 52.6 reduce-scatter.4

commit v4 on v3

--- a/solution.py
+++ b/solution.py
@@ -33,16 +33,18 @@
     return jnp.cos(angle), jnp.sin(angle)
 
 
-def spread_filter(filter_spectra, own):
-    _, _, row_count, channels = filter_spectra.shape
+def to_share(filter_part):
+    parts, row_count, channels = filter_part.shape
     seq_count = lax.axis_size("seq")
-    pieces = filter_spectra[:, own].reshape(2, row_count, seq_count, channels // seq_count)
-    return lax.all_to_all(
-        pieces.transpose(2, 0, 1, 3), "seq", split_axis=0, concat_axis=0, tiled=True
-    )
-
-
-def long_filter(cos_ref, sin_ref, x_ref, ct_ref, st_ref, h0_ref, h1_ref, table_ref, out_ref, acc, left, right):
+    pieces = filter_part.reshape(parts, row_count, seq_count, channels // seq_count)
+    return pieces.transpose(2, 0, 1, 3)
+
+
+def exchanged(pieces):
+    return lax.all_to_all(pieces, "seq", split_axis=0, concat_axis=0, tiled=True)
+
+
+def long_filter(cos_ref, sin_ref, x_ref, ct_ref, st_ref, hr_ref, hi_ref, table_ref, out_ref, acc, left, right):
     blocks, row_count, share = x_ref.shape
     step = pl.program_id(0)
     chunk, tile = 64, 512
@@ -76,8 +78,7 @@
         for q in range(2):
             lanes = slice(q * share, (q + 1) * share)
             a, b = real[:, lanes], imag[:, lanes]
-            h_ref = (h0_ref, h1_ref)[q]
-            hr, hi = h_ref[0, 0, rows, :].astype(F32), h_ref[0, 1, rows, :].astype(F32)
+            hr, hi = hr_ref[q, 0, rows, :].astype(F32), hi_ref[q, 0, rows, :].astype(F32)
             right[rows, lanes] = (a * hr - b * hi).astype(BF16)
             right[below, lanes] = (-(a * hi + b * hr)).astype(BF16)
 
@@ -106,15 +107,15 @@
         out_ref[...] = (acc[...] * scale).astype(BF16)
 
 
-def call_long_filter(cos_block, sin_block, columns, cos_twist, sin_twist, first, second, table):
+def call_long_filter(cos_block, sin_block, columns, cos_twist, sin_twist, hr, hi, table):
     blocks, row_count, share = columns.shape
     whole = lambda *shape: pl.BlockSpec(shape, lambda k: (0,) * len(shape))
     twist = pl.BlockSpec((2, row_count, share), lambda k: (k, 0, 0))
-    piece = pl.BlockSpec((1, 2, row_count, share), lambda k: (k, 0, 0, 0))
-    flops = 2 * blocks * 2 * (2 * row_count) ** 2 * (2 * share)
+    last = hi.shape[1] - 1
+    flops = blocks * 2 * (2 * row_count) ** 2 * (2 * share)
     return pl.pallas_call(
         long_filter,
-        grid=(blocks,),
+        grid=(blocks // 2,),
         out_shape=jax.ShapeDtypeStruct(columns.shape, BF16),
         in_specs=[
             pl.BlockSpec(memory_space=pltpu.SMEM),
@@ -122,8 +123,8 @@
             whole(blocks, row_count, share),
             twist,
             twist,
-            piece,
-            piece,
+            pl.BlockSpec((2, 1, row_count, share), lambda k: (k, 0, 0, 0)),
+            pl.BlockSpec((2, 1, row_count, share), lambda k: (k, last, 0, 0)),
             whole(2 * row_count, 2 * row_count),
         ],
         out_specs=whole(blocks, row_count, share),
@@ -133,8 +134,8 @@
             pltpu.VMEM((2 * row_count, 2 * share), BF16),
         ],
         compiler_params=pltpu.CompilerParams(vmem_limit_bytes=56 * 2**20),
-        cost_estimate=pl.CostEstimate(flops=flops, bytes_accessed=40 * 2**20, transcendentals=0),
-    )(cos_block, sin_block, columns, cos_twist, sin_twist, first, second, table)
+        cost_estimate=pl.CostEstimate(flops=flops, bytes_accessed=24 * 2**20, transcendentals=0),
+    )(cos_block, sin_block, columns, cos_twist, sin_twist, hr, hi, table)
 
 
 def on_device(tokens, w_in, w_short, skip_gain, filter_spectra, w_out):
@@ -145,10 +146,24 @@
     share = channels // seq_count
     fft_length = bin_count * row_count
 
-    first_filter = spread_filter(filter_spectra, 0)
+    first_filter = exchanged(to_share(filter_spectra[:, 0]))
+    classes = jnp.arange(bin_count, dtype=jnp.int32)
+    cos_block, sin_block = phases(classes, jnp.arange(seq_count, dtype=jnp.int32), bin_count)
+    cos_twist, sin_twist = phases(classes, jnp.arange(row_count, dtype=jnp.int32), fft_length)
+    cos_twist, sin_twist = cos_twist[:, :, None], sin_twist[:, :, None]
+    twist_shape = (seq_count, row_count, share)
+    twists = [
+        jnp.broadcast_to(table[parity::2], twist_shape)
+        for parity in range(2)
+        for table in (cos_twist, sin_twist)
+    ]
+
     gathered = lax.all_gather(tokens, "ch", axis=1, tiled=True)
-    gathered, first_filter = lax.optimization_barrier((gathered, first_filter))
-    second_filter = spread_filter(filter_spectra, 1)
+    late = to_share(filter_spectra[1:, 1])
+    gathered, first_filter, twists, late = lax.optimization_barrier(
+        (gathered, first_filter, twists, late)
+    )
+    second_real = exchanged(to_share(filter_spectra[:1, 1]))
     projected = [
         jnp.dot(gathered, w_in[:, s], preferred_element_type=F32).astype(BF16) for s in range(3)
     ]
@@ -160,7 +175,7 @@
         return taps[0] * extended[2:] + taps[1] * extended[1:-1] + taps[2] * extended[:-2]
 
     signal = (stream(0) * stream(2)).astype(BF16)
-    signal, second_filter = lax.optimization_barrier((signal, second_filter))
+    signal, second_real = lax.optimization_barrier((signal, second_real))
     second_gate = stream(1)
 
     columns = lax.all_to_all(
@@ -170,20 +185,24 @@
         concat_axis=0,
         tiled=True,
     )
-    classes = jnp.arange(bin_count, dtype=jnp.int32)
-    cos_block, sin_block = phases(classes, jnp.arange(seq_count, dtype=jnp.int32), bin_count)
-    cos_twist, sin_twist = phases(classes, jnp.arange(row_count, dtype=jnp.int32), fft_length)
-    twist_shape = (bin_count, row_count, share)
-    convolved = call_long_filter(
-        cos_block,
-        sin_block,
-        columns,
-        jnp.broadcast_to(cos_twist[:, :, None], twist_shape),
-        jnp.broadcast_to(sin_twist[:, :, None], twist_shape),
-        first_filter,
-        second_filter,
-        jnp.asarray(dense_transform(row_count)),
-    )
+    columns, late = lax.optimization_barrier((columns, late))
+    second_imag = exchanged(late)
+    table = jnp.asarray(dense_transform(row_count))
+    filters = ((first_filter, first_filter), (second_real, second_imag))
+    shares = [
+        call_long_filter(
+            cos_block[parity::2],
+            sin_block[parity::2],
+            columns,
+            twists[2 * parity],
+            twists[2 * parity + 1],
+            *filters[parity],
+            table,
+        )
+        for parity in range(2)
+    ]
+    convolved = (shares[0].astype(F32) + shares[1].astype(F32)).astype(BF16)
+
     owners = lax.axis_size("ch")
     half = row_count // (2 * owners)
 
@@ -193,21 +212,16 @@
         return picked.reshape(array.shape[:axis] + (owners * half,) + array.shape[axis + 1 :])
 
     outs = []
+    backs = [exchanged(rows_of(convolved, h, 1)) for h in range(2)]
     for h in range(2):
-        back = lax.all_to_all(
-            rows_of(convolved, h, 1), "seq", split_axis=0, concat_axis=0, tiled=True
-        )
+        back = backs[h]
+        if h:
+            back, product = lax.optimization_barrier((back, product[:16, :128]))
         back = back.transpose(1, 0, 2).reshape(owners * half, channels).astype(F32)
         response = back + skip_gain * rows_of(signal, h, 0).astype(F32)
         gated_out = (rows_of(second_gate, h, 0) * response).astype(BF16)
-        outs.append(
-            lax.psum_scatter(
-                jnp.dot(gated_out, w_out, preferred_element_type=F32).astype(BF16),
-                "ch",
-                scatter_dimension=0,
-                tiled=True,
-            )
-        )
+        product = jnp.dot(gated_out, w_out, preferred_element_type=F32).astype(BF16)
+        outs.append(lax.psum_scatter(product, "ch", scatter_dimension=0, tiled=True))
     return jnp.concatenate(outs, 0)
 
 

time: 565 us -> 536 us (0.949)
  waiting for transfers between devices: 308 us -> 214 us
  blocking collectives: 0 us -> 56.1 us
  Pallas kernels: 71.5 us -> 78.4 us
    all_to_all x5, waiting for transfers between devices: 210 us -> 116 us  [exchanged(): lax.all_to_all(pieces, 'seq', split_axis=0, concat_axis=0, tiled=True)]
    all_to_all x0 -> x1, blocking collectives: none -> 56.1 us  [on_device(): lax.all_to_all(signal.reshape(row_count, seq_count, share).transpose(1, 0...]
    pallas_call x1 -> x2, Pallas kernels: 71.5 us -> 78.4 us  [call_long_filter(): pl.pallas_call(long_filter, grid=(blocks // 2,), out_shape=jax.ShapeDtype...]
    slice x1 -> x10, local copies, waits for them, and re-layouts: 5.91 us -> 11.8 us  [the longest x1 4.71 us: on_device(): second_real = exchanged(to_share(filter_spectra[:1, 1]))]
    another operation x2 -> x3, local copies, waits for them, and re-layouts: 13.1 us -> 11.7 us  [to_share(): filter_part.reshape(parts, row_count, seq_count, channels // seq_count)]
    unnamed x14 -> x19, local copies, waits for them, and re-layouts: 13.7 us -> 13.2 us
  transfers between devices with their start and end apart: 9 -> 9, of which waited for: 8 -> 7; matrix products, arithmetic and copies ran while one was open for 19% -> 22% of each run, Pallas kernels for 0% -> 7%
where the time goes in v4:
time: 536 us; the launch traced here: 535 us
  waiting for transfers between devices  214 us (40%)
  Pallas kernels  78.4 us (15%)
  local copies, waits for them, and re-layouts  72.3 us (13%)
  blocking collectives  56.1 us (10%)
  matrix products  53.4 us (10%)
  starting transfers between devices  25.6 us (5%)
  other arithmetic  21 us (4%)
  between operations  13.4 us (2%)
    all_to_all x5, waiting for transfers between devices, exchanged(): lax.all_to_all(pieces, 'seq', split_axis=0, concat_axis=0, tiled=True)  116 us
    reduce_scatter x2, waiting for transfers between devices, on_device(): lax.psum_scatter(product, 'ch', scatter_dimension=0, tiled=True)  97 us
    pallas_call x2, Pallas kernels, call_long_filter(): pl.pallas_call(long_filter, grid=(blocks // 2,), out_shape=jax.ShapeDtype...  78.4 us
    all_to_all x1, blocking collectives, on_device(): lax.all_to_all(signal.reshape(row_count, seq_count, share).transpose(1, 0...  56.1 us
    dot_general x3, matrix products, on_device(): jnp.dot(gathered, w_in[:, s], preferred_element_type=F32).astype(BF16)  34.3 us
    all_to_all x5, starting transfers between devices, exchanged(): lax.all_to_all(pieces, 'seq', split_axis=0, concat_axis=0, tiled=True)  23 us
    dot_general x2, matrix products, on_device(): product = jnp.dot(gated_out, w_out, preferred_element_type=F32).astype(BF16)  19 us
    unnamed x19, local copies, waits for them, and re-layouts  13.2 us
  transfers between devices with their start and end apart: 9, of which 7 were waited for; matrix products, arithmetic and copies ran while one was open for 22% of the time, Pallas kernels for 7%

profile of v4, /device:TPU:0, one launch (start us, length us, event | category | flops | bytes accessed | tf_op | source)
XLA Modules:
  0.0 534.7 jit_solution(6003730843541026946)
XLA Ops:
  7.3 4.6 slice.155
  11.8 6.3 %copy.28 = bf16[2,1,1024,1024]{2,3,0,1:T(8,128)(2,1)} copy(bf16[2,1,1024,1024]{3,2,1,0:T(8,128)(2,1)} %slice.155) | data formatting | bytes 8388608
  18.1 6.8 %copy.9 = bf16[2,1024,8,128]{3,1,0,2:T(8,128)(2,1)} copy(bf16[2,1024,8,128]{1,3,2,0:T(8,128)(2,1)} %bitcast.86) | data formatting | bytes 8388608 | tf_op jit(solution)/shard_map/reshape;squeeze | solution.py:39
  24.9 6.3 %all-to-all-start = ((bf16[8,2,1024,128]{3,2,1,0:T(8,128)(2,1)}), bf16[8,2,1024,128]{3,2,1,0:T(8,128)(2,1)}, u32[]{:S(2)}, u32[]{:S(2)}) async-start(bf16[8,2,1024,128]{3,2,1,0:T(8,128)(2,1)} %bitcast.85), calls=%async_computation | async-start | bytes 8388608 | tf_op jit(solution)/shard_map/all_to_all | solution.py:44
  31.8 4.7 fusion.46
  36.5 2.9 copy.29
  39.4 2.5 copy.11
  41.8 2.9 copy.30
  44.7 2.4 copy.14
  47.1 78.2 %all-to-all-done.hr_ref.hi_ref = bf16[8,2,1024,128]{3,2,1,0:T(8,128)(2,1)} async-done(((bf16[8,2,1024,128]{3,2,1,0:T(8,128)(2,1)}), bf16[8,2,1024,128]{3,2,1,0:T(8,128)(2,1)}, u32[]{:S(2)}, u32[]{:S(2)}) %all-to-all-start) | async-done | bytes 4194336 | tf_op jit(solution)/shard_map/all_to_all | solution.py:44
  125.3 4.5 all-to-all-start.1
  129.9 2.8 broadcast_in_dim.17.ct_ref
  132.7 2.6 broadcast_in_dim.19.st_ref
  135.3 2.7 broadcast_in_dim.41.ct_ref
  138.0 2.6 broadcast_in_dim.43.st_ref
  140.6 11.2 %fusion.24 = bf16[1024,1024]{1,0:T(8,128)(2,1)S(1)} fusion(bf16[1024,4096]{1,0:T(8,128)(2,1)S(1)} %bitcast.112, bf16[4096,3,1024]{2,0,1:T(8,128)(2,1)} %param.8), kind=kOutput, calls=%fused_computation.40 | convolution fusion | flops 8590983168 | bytes 18874368 | tf_op jit(solution)/shard_map/dot_general | solution.py:168
  151.8 11.9 %fusion.27 = bf16[1024,1024]{1,0:T(8,128)(2,1)S(1)} fusion(bf16[1024,4096]{1,0:T(8,128)(2,1)S(1)} %bitcast.112, bf16[4096,3,1024]{2,0,1:T(8,128)(2,1)} %param.8), kind=kOutput, calls=%fused_computation.41 | convolution fusion | flops 8590983168 | bytes 18874368 | tf_op jit(solution)/shard_map/dot_general | solution.py:168
  163.8 11.2 %fusion.21 = bf16[1024,1024]{1,0:T(8,128)(2,1)S(1)} fusion(bf16[1024,4096]{1,0:T(8,128)(2,1)S(1)} %bitcast.112, bf16[4096,3,1024]{2,0,1:T(8,128)(2,1)} %param.8), kind=kOutput, calls=%fused_computation.39 | convolution fusion | flops 8590983168 | bytes 18874368 | tf_op jit(solution)/shard_map/dot_general | solution.py:168
  175.1 2.3 collective-permute-start
  179.2 2.7 fusion.11
  181.9 2.6 copy.15
  184.5 3.9 copy.16
  188.4 56.1 %all_to_all.30.x_ref = bf16[8,1024,128]{2,1,0:T(8,128)(2,1)} all-to-all(bf16[8,1024,128]{2,1,0:T(8,128)(2,1)} %bitcast.92), channel_id=1, replica_groups=mesh['seq'=8,'ch'=4] {'seq'}, dimensions={0} | all-to-all | bytes 4194304 | tf_op jit(solution)/shard_map/all_to_all | solution.py:181
  244.5 4.4 all-to-all-start.3
  251.4 39.0 %shard_map.73 = bf16[8,1024,128]{2,1,0:T(8,128)(2,1)} custom-call(f32[8,8]{1,0:T(8,128)} %slice.174.cos_ref, f32[8,8]{1,0:T(8,128)} %slice.175.sin_ref, bf16[8,1024,128]{2,1,0:T(8,128)(2,1)} %all_to_all.30.x_ref, f32[8,1024,128]{2,1,0:T(8,128)} %broadcast_in_dim.17.ct_ref, f32[8,1024,128]{2,1,0:T(8,128)} %broadcast_in_dim.19.st_ref, ...), custom_call_target="tpu_custom_call" | custom-call | flops 17179869184 | bytes 25165824 | tf_op jit(solution)/shard_map/pallas_call | solution.py:116
  290.4 7.5 %all-to-all-done.3.hi_ref = bf16[8,1,1024,128]{3,2,1,0:T(8,128)(2,1)} async-done(((bf16[8,1,1024,128]{3,2,1,0:T(8,128)(2,1)}), bf16[8,1,1024,128]{3,2,1,0:T(8,128)(2,1)}, u32[]{:S(2)}, u32[]{:S(2)}) %all-to-all-start.3) | async-done | bytes 2097184 | tf_op jit(solution)/shard_map/all_to_all | solution.py:44
  297.9 39.4 %shard_map.74 = bf16[8,1024,128]{2,1,0:T(8,128)(2,1)} custom-call(f32[8,8]{1,0:T(8,128)} %slice.191.cos_ref, f32[8,8]{1,0:T(8,128)} %slice.192.sin_ref, bf16[8,1024,128]{2,1,0:T(8,128)(2,1)} %all_to_all.30.x_ref, f32[8,1024,128]{2,1,0:T(8,128)} %broadcast_in_dim.41.ct_ref, f32[8,1024,128]{2,1,0:T(8,128)} %broadcast_in_dim.43.st_ref, ...), custom_call_target="tpu_custom_call" | custom-call | flops 17179869184 | bytes 25165824 | tf_op jit(solution)/shard_map/pallas_call | solution.py:116
  337.4 2.1 add_convert_fusion
  342.1 3.6 all-to-all-start.5
  345.6 1.6 fusion.49
  347.2 2.3 copy.23
  349.5 22.6 %all-to-all-done.5 = bf16[8,512,128]{1,2,0:T(8,128)(2,1)S(1)} async-done(((bf16[8,512,128]{1,2,0:T(8,128)(2,1)}), bf16[8,512,128]{1,2,0:T(8,128)(2,1)S(1)}, u32[]{:S(2)}, u32[]{:S(2)}) %all-to-all-start.5) | async-done | bytes 1048608 | tf_op jit(solution)/shard_map/all_to_all | solution.py:44
  372.1 4.2 all-to-all-start.4
  376.7 1.5 bitcast_convert_fusion.1
  378.2 1.9 copy.24
  380.0 1.5 bitcast_convert_fusion
  381.5 1.9 copy.27
  383.4 2.2 maximum_convert_fusion
  386.8 2.4 fusion.47
  389.2 3.0 copy.22
  392.2 2.9 copy.25
  395.1 7.9 %all-to-all-done.4 = bf16[8,512,128]{1,2,0:T(8,128)(2,1)} async-done(((bf16[8,512,128]{1,2,0:T(8,128)(2,1)}), bf16[8,512,128]{1,2,0:T(8,128)(2,1)}, u32[]{:S(2)}, u32[]{:S(2)}) %all-to-all-start.4) | async-done | bytes 1048608 | tf_op jit(solution)/shard_map/all_to_all | solution.py:44
  403.0 4.9 fusion.20
  407.9 9.5 %convolution_convert_fusion.1 = bf16[512,4096]{1,0:T(8,128)(2,1)} fusion(bf16[512,1024]{0,1:T(8,128)(2,1)S(1)} %get-tuple-element.47, bf16[1024,4096]{1,0:T(8,128)(2,1)} %param.12), kind=kOutput, calls=%fused_computation.10 | convolution fusion | flops 4297064448 | bytes 13631488 | tf_op jit(solution)/shard_map/dot_general | solution.py:223
  418.6 9.6 %convolution_convert_fusion = bf16[512,4096]{1,0:T(8,128)(2,1)} fusion(bf16[512,1024]{0,1:T(8,128)(2,1)S(1)} %copy-done.3, bf16[1024,4096]{1,0:T(8,128)(2,1)} %param.12), kind=kOutput, calls=%fused_computation.9 | convolution fusion | flops 4297064448 | bytes 13631488 | tf_op jit(solution)/shard_map/dot_general | solution.py:223
  428.2 41.0 %reduce-scatter.3.cloned.1.call-done = bf16[128,4096]{1,0:T(8,128)(2,1)} async-done(((bf16[512,4096]{1,0:T(8,128)(2,1)}), bf16[128,4096]{1,0:T(8,128)(2,1)}) %reduce-scatter.3.cloned.1.call-update) | async-done | bytes 1048592 | tf_op jit(solution)/shard_map/reduce_scatter | solution.py:224
  469.1 56.0 %reduce-scatter.5.cloned.1.call-done = bf16[128,4096]{1,0:T(8,128)(2,1)} async-done(((bf16[512,4096]{1,0:T(8,128)(2,1)}), bf16[128,4096]{1,0:T(8,128)(2,1)}) %reduce-scatter.5.cloned.1.call-update) | async-done | bytes 1048592 | tf_op jit(solution)/shard_map/reduce_scatter | solution.py:224
  525.1 3.1 pad_maximum_fusion
  (48 shorter events, 11.0 us)
Async XLA Ops:
  6.5 123.4 %all-gather.2.cloned.1.call-start = ((), (), s32[]{:S(2)}) async-start(), calls=%async_computation.8 | async-start | bytes 10485760 | tf_op jit(solution)/shard_map/all_gather | solution.py:161
  24.9 100.4 %all-to-all-start = ((bf16[8,2,1024,128]{3,2,1,0:T(8,128)(2,1)}), bf16[8,2,1024,128]{3,2,1,0:T(8,128)(2,1)}, u32[]{:S(2)}, u32[]{:S(2)}) async-start(bf16[8,2,1024,128]{3,2,1,0:T(8,128)(2,1)} %bitcast.85), calls=%async_computation | async-start | bytes 8388608 | tf_op jit(solution)/shard_map/all_to_all | solution.py:44
  125.3 56.6 %all-to-all-start.1 = ((bf16[8,1,1024,128]{3,2,1,0:T(8,128)(2,1)}), bf16[8,1,1024,128]{3,2,1,0:T(8,128)(2,1)}, u32[]{:S(2)}, u32[]{:S(2)}) async-start(bf16[8,1,1024,128]{3,2,1,0:T(8,128)(2,1)} %bitcast.29), calls=%async_computation.1 | async-start | bytes 4194304 | tf_op jit(solution)/shard_map/all_to_all | solution.py:44
  129.9 10.7 %slice-start = ((s8[8388608]{0:T(1024)(128)(4,1)}), s8[4194304]{0:T(1024)(128)(4,1)S(1)}, s32[]{:S(2)}) async-start(s8[8388608]{0:T(1024)(128)(4,1)} %bitcast.111), calls=%async_computation.11 | async-start | bytes 8388608
  135.3 5.3 slice-start.1
  151.8 23.2 %copy-start.1 = (bf16[1024,1024]{1,0:T(8,128)(2,1)}, bf16[1024,1024]{1,0:T(8,128)(2,1)S(1)}, u32[]{:S(2)}) copy-start(bf16[1024,1024]{1,0:T(8,128)(2,1)S(1)} %fusion.24) | copy-start | bytes 6291460
  163.8 13.6 %copy-start.4 = (f32[3,3,1024]{2,1,0:T(4,128)S(1)}, f32[3,3,1024]{2,1,0:T(4,128)}, u32[]{:S(2)}) copy-start(f32[3,3,1024]{2,1,0:T(4,128)} %param.9) | copy-start | bytes 110596
  175.1 2.9 collective-permute-start
  244.5 53.4 %all-to-all-start.3 = ((bf16[8,1,1024,128]{3,2,1,0:T(8,128)(2,1)}), bf16[8,1,1024,128]{3,2,1,0:T(8,128)(2,1)}, u32[]{:S(2)}, u32[]{:S(2)}) async-start(bf16[8,1,1024,128]{3,2,1,0:T(8,128)(2,1)} %bitcast.89), calls=%async_computation.3 | async-start | bytes 4194304 | tf_op jit(solution)/shard_map/all_to_all | solution.py:44
  297.9 39.4 %copy-start.2 = (bf16[8,1024,128]{2,1,0:T(8,128)(2,1)S(1)}, bf16[8,1024,128]{2,1,0:T(8,128)(2,1)}, u32[]{:S(2)}) copy-start(bf16[8,1024,128]{2,1,0:T(8,128)(2,1)} %shard_map.73) | copy-start | bytes 6291460
  342.1 30.1 %all-to-all-start.5 = ((bf16[8,512,128]{1,2,0:T(8,128)(2,1)}), bf16[8,512,128]{1,2,0:T(8,128)(2,1)S(1)}, u32[]{:S(2)}, u32[]{:S(2)}) async-start(bf16[8,512,128]{1,2,0:T(8,128)(2,1)} %copy.26), calls=%async_computation.6 | async-start | bytes 2097152 | tf_op jit(solution)/shard_map/all_to_all | solution.py:44
  372.1 30.8 %all-to-all-start.4 = ((bf16[8,512,128]{1,2,0:T(8,128)(2,1)}), bf16[8,512,128]{1,2,0:T(8,128)(2,1)}, u32[]{:S(2)}, u32[]{:S(2)}) async-start(bf16[8,512,128]{1,2,0:T(8,128)(2,1)} %copy.23), calls=%async_computation.4 | async-start | bytes 2097152 | tf_op jit(solution)/shard_map/all_to_all | solution.py:44
  376.4 92.7 %reduce-scatter.3.cloned.1.call-start = ((), (), s32[]{:S(2)}) async-start(), calls=%async_computation.9 | async-start | bytes 5242880 | tf_op jit(solution)/shard_map/reduce_scatter | solution.py:224
  389.2 13.8 %copy-start = (f32[512,1024]{0,1:T(8,128)S(1)}, f32[512,1024]{0,1:T(8,128)}, u32[]{:S(2)}) copy-start(f32[512,1024]{0,1:T(8,128)} %copy.24) | copy-start | bytes 6291460
  389.2 13.8 %copy-start.5 = (f32[1024]{0:T(1024)S(1)}, f32[1024]{0:T(1024)}, u32[]{:S(2)}) copy-start(f32[1024]{0:T(1024)} %param.10) | copy-start | bytes 12292
  417.4 1.2 copy-start.3
  417.4 107.7 %reduce-scatter.5.cloned.1.call-start = ((), (), s32[]{:S(2)}) async-start(), calls=%async_computation.10 | async-start | bytes 5242880 | tf_op jit(solution)/shard_map/reduce_scatter | solution.py:224
Sparse Core Ops, SparseCore 0:
  9.2 90.2 all-gather.1
  417.5 51.5 reduce-scatter.2
  472.4 52.6 reduce-scatter.4
